TPU v7x, 32 devices: a whole 2x2x4 slice. The times are simulated.
32 devices in a mesh: band: 2 (over x), inp: 16 (over z, y, core).
Axes of the slice: x: 2, y: 2, z: 4, core: 2. Of those that a mesh axis runs over, the one named last changes fastest.
Arguments:
- samples: bfloat16 [256, 268288], P(('band', 'inp')), parts along dimension 0, may hold values from -128 to 127, as said below
- taps: int32 [4, 2048], replicated, may hold values from -127 to 127
Outputs:
- visibilities: bfloat16 [64, 2, 128, 128], P(('band', 'inp')), parts along dimension 0
There are 2 independent parts, one for each index of `band`. A program takes and returns all parts, laid end to end along the dimension named above; an argument that names none is the same for every part. Nothing has to cross between parts.
Inputs may be any that keep to these rules, and one draw needn't show every extreme that they name: `samples`: every sample is an integer.
All inputs are finite; a program needn't handle non-finite values.
Results may differ from a plain program's by a relative error of at most 0.0074.
Values may be sent and summed in bfloat16 or wider, within the bound.
A program may use at most 64 MiB of HBM per device.

v0:
```python
import math

import jax
import jax.numpy as jnp
from jax import lax
from jax.sharding import PartitionSpec as P

CH_DEV = 2
NFFT = 2048
TAPS = 4
FIRST_CH = 256
SPEC = 128


def layout_table(groups):
    sample_index = jnp.arange(NFFT, dtype=jnp.int32)[:, None]
    column = jnp.arange(2 * CH_DEV * groups, dtype=jnp.int32)[None, :]
    local_channel = column // (2 * groups)
    group_index = column // 2 % groups
    is_imag = column % 2
    channel = FIRST_CH + group_index * CH_DEV + local_channel
    phase = (sample_index * channel % NFFT).astype(jnp.float32) * (2.0 * math.pi / NFFT)
    scale_factor = 2.0 ** (-19)
    table = jnp.where(is_imag == 0, jnp.cos(phase) * scale_factor, -jnp.sin(phase) * scale_factor)
    return table.astype(jnp.bfloat16)


def correlate(turned):
    norm_factor = 1.0 / math.sqrt(SPEC)

    def single(block):
        rotated = jnp.stack([block[:, 1], -block[:, 0]], axis=1)
        stacked = jnp.stack([block, rotated])
        product = jnp.einsum(
            "qarxs,brys->qaxby", stacked, block, preferred_element_type=jnp.float32
        )
        width = block.shape[0] * block.shape[2]
        return (product.reshape(2, width, width) * norm_factor).astype(jnp.bfloat16)

    return lax.map(single, turned)


def per_device(samples, taps):
    groups = lax.axis_size("inp")
    per_dev = samples.shape[0]
    frames = samples.reshape(per_dev, SPEC + TAPS - 1, NFFT)
    tap_values = taps.astype(jnp.float32)
    filtered = tap_values[0] * frames[:, 0:SPEC, :].astype(jnp.float32)
    for tap_index in range(1, TAPS):
        filtered = filtered + tap_values[tap_index] * frames[
            :, tap_index : tap_index + SPEC, :
        ].astype(jnp.float32)
    flat_rows = filtered.reshape(per_dev * SPEC, NFFT).astype(jnp.bfloat16)
    dft_table = layout_table(groups)
    voltages = lax.dot_general(
        dft_table, flat_rows, (((0,), (1,)), ((), ())), preferred_element_type=jnp.float32
    ).astype(jnp.bfloat16)
    outgoing = voltages.reshape(CH_DEV, groups, 2, per_dev, SPEC)
    result = correlate(lax.all_to_all(outgoing, "inp", split_axis=1, concat_axis=1, tiled=True))
    return result


def solution(mesh):
    placed = (P(("band", "inp"), None), P())
    return jax.shard_map(
        per_device,
        mesh=mesh,
        in_specs=placed,
        out_specs=P(("band", "inp"), None, None, None),
        check_vma=False,
    )
```

profile of v0, /device:TPU:0, one launch (start us, length us, event | category | flops | bytes accessed | tf_op | source)
XLA Modules:
  0.0 34.0 jit_solution(1629840590919251531)
XLA Ops:
  0.0 0.8 %convert_element_type.35 = f32[4,2048]{1,0:T(4,128)S(1)} convert(s32[4,2048]{1,0:T(4,128)} %param.5) | non-fusion elementwise | flops 8192 | bytes 65536 | tf_op jit(solution)/shard_map/convert_element_type | solution.py:47
  0.8 8.5 %add_convert_fusion = bf16[8,128,2048]{2,0,1:T(8,128)(2,1)S(1)} fusion(bf16[8,131,2048]{2,0,1:T(8,128)(2,1)} %bitcast.53, f32[2048]{0:T(1024)S(1)} %bitcast.57, f32[2048]{0:T(1024)S(1)} %bitcast.58, f32[2048]{0:T(1024)S(1)} %bitcast.59, f32[2048]{0:T(1024)S(1)} %bitcast.56), kind=kLoop, calls=%fused_computation.14 | loop fusion | flops 25165824 | bytes 21004288 | tf_op jit(solution)/shard_map/convert_element_type | solution.py:53
  9.3 2.3 %copy.7 = bf16[8,128,2048]{2,1,0:T(8,128)(2,1)S(1)} copy(bf16[8,128,2048]{2,0,1:T(8,128)(2,1)S(1)} %add_convert_fusion) | data formatting | bytes 8388608 | tf_op jit(solution)/shard_map/convert_element_type | solution.py:53
  11.6 5.1 %fusion.8 = bf16[8,8,8,128]{3,1,2,0:T(8,128)(2,1)S(1)} fusion(bf16[1024,2048]{1,0:T(8,128)(2,1)S(1)} %bitcast.54, s32[64]{0:T(128)S(1)} %fusion.22, pred[64]{0:T(512)(128)(4,1)S(1)} %fusion.23), kind=kOutput, calls=%fused_computation.19 | convolution fusion | flops 270991360 | bytes 4325696 | tf_op jit(solution)/shard_map/dot_general | solution.py:55
  16.8 0.7 %copy.8 = bf16[2,16,2,8,128]{4,3,2,0,1:T(8,128)(2,1)} copy(bf16[2,16,2,8,128]{4,3,2,1,0:T(8,128)(2,1)S(1)} %bitcast.55) | data formatting | bytes 262144 | tf_op jit(solution)/shard_map/reshape | solution.py:58
  17.5 7.4 %all-to-all-start = ((bf16[2,16,2,8,128]{4,3,2,0,1:T(8,128)(2,1)}), bf16[2,16,2,8,128]{4,3,2,0,1:T(8,128)(2,1)S(1)}, u32[]{:S(2)}, u32[]{:S(2)}) async-start(bf16[2,16,2,8,128]{4,3,2,0,1:T(8,128)(2,1)} %copy.8), calls=%async_computation | async-start | bytes 262144 | tf_op jit(solution)/shard_map/all_to_all | solution.py:59
  24.9 7.9 %all-to-all-done = bf16[2,16,2,8,128]{4,3,2,0,1:T(8,128)(2,1)S(1)} async-done(((bf16[2,16,2,8,128]{4,3,2,0,1:T(8,128)(2,1)}), bf16[2,16,2,8,128]{4,3,2,0,1:T(8,128)(2,1)S(1)}, u32[]{:S(2)}, u32[]{:S(2)}) %all-to-all-start) | async-done | bytes 131104 | tf_op jit(solution)/shard_map/all_to_all | solution.py:59
  32.8 0.6 %while.10 = (s32[]{:T(128)}, bf16[2,2,128,128]{3,2,1,0:T(8,128)(2,1)S(1)}, bf16[2,16,2,8,128]{4,3,2,0,1:T(8,128)(2,1)S(1)}, s32[]{:T(128)}) while((s32[]{:T(128)}, bf16[2,2,128,128]{3,2,1,0:T(8,128)(2,1)S(1)}, bf16[2,16,2,8,128]{4,3,2,0,1:T(8,128)(2,1)S(1)}, s32[]{:T(128)}) %tuple.28), condition=%wide.region_1.2_spmd, body=%wide.region_0.1_spmd.sunk | while | flops 16957440 | bytes 720957 | solution.py:40
  32.8 0.2 fusion.43
  33.1 0.2 fusion.43
  33.4 0.0 copy-start
  33.4 0.6 %copy-done = bf16[2,2,128,128]{3,2,1,0:T(8,128)(2,1)} copy-done((bf16[2,2,128,128]{3,2,1,0:T(8,128)(2,1)}, bf16[2,2,128,128]{3,2,1,0:T(8,128)(2,1)S(1)}, u32[]{:S(2)}) %copy-start) | copy-done | bytes 131096
  (11 shorter events, 0.1 us)
Async XLA Ops:
  17.5 15.3 %all-to-all-start = ((bf16[2,16,2,8,128]{4,3,2,0,1:T(8,128)(2,1)}), bf16[2,16,2,8,128]{4,3,2,0,1:T(8,128)(2,1)S(1)}, u32[]{:S(2)}, u32[]{:S(2)}) async-start(bf16[2,16,2,8,128]{4,3,2,0,1:T(8,128)(2,1)} %copy.8), calls=%async_computation | async-start | bytes 262144 | tf_op jit(solution)/shard_map/all_to_all | solution.py:59
  33.4 0.7 %copy-start = (bf16[2,2,128,128]{3,2,1,0:T(8,128)(2,1)}, bf16[2,2,128,128]{3,2,1,0:T(8,128)(2,1)S(1)}, u32[]{:S(2)}) copy-start(bf16[2,2,128,128]{3,2,1,0:T(8,128)(2,1)S(1)} %get-tuple-element.80) | copy-start | bytes 393220
where the time goes:
time: 34.3 us; the launch traced here: 34 us
  other arithmetic  9.34 us (27%)
  waiting for transfers between devices  7.93 us (23%)
  starting transfers between devices  7.39 us (22%)
  matrix products  5.53 us (16%)
  local copies, waits for them, and re-layouts  3.7 us (11%)
    convert_element_type x1, other arithmetic, per_device(): flat_rows = filtered.reshape(per_dev * SPEC, NFFT).astype(jnp.bfloat16)  8.52 us
    all_to_all x1, waiting for transfers between devices, per_device(): lax.all_to_all(outgoing, 'inp', split_axis=1, concat_axis=1, tiled=True)  7.93 us
    all_to_all x1, starting transfers between devices, per_device(): lax.all_to_all(outgoing, 'inp', split_axis=1, concat_axis=1, tiled=True)  7.39 us
    dot_general x1, matrix products, per_device(): lax.dot_general(dft_table, flat_rows, (((0,), (1,)), ((), ())), preferred...  5.13 us
    convert_element_type x1, local copies, waits for them, and re-layouts, per_device(): flat_rows = filtered.reshape(per_dev * SPEC, NFFT).astype(jnp.bfloat16)  2.3 us
    convert_element_type x1, other arithmetic, per_device(): tap_values = taps.astype(jnp.float32)  0.76 us
  transfers between devices with their start and end apart: 1, of which 1 were waited for; matrix products, arithmetic and copies ran while one was open for 0% of the time, Pallas kernels for 0%

commit v1 on v0

v1 whole, which is shorter than its diff:
```python
import functools
import math

import jax
import jax.numpy as jnp
import numpy as np
from jax import lax
from jax.experimental import pallas as pl
from jax.experimental.pallas import tpu as pltpu
from jax.sharding import PartitionSpec as P

CH_DEV = 2
NFFT = 2048
TAPS = 4
FIRST_CH = 256
SPEC = 128
INP_DEV = 8
FRAMES = SPEC + TAPS - 1
BLOCK = 16
COLS = BLOCK * CH_DEV * 2
CHUNKS = ((0, 34), (34, 68), (68, 100), (100, 131))
PAD_ROWS = (FRAMES + 1) * INP_DEV
BLOCK_ROWS = CH_DEV * 2 * INP_DEV


def dft_table(groups):
    n = np.arange(NFFT, dtype=np.int64)[None, :]
    row = np.arange(groups * CH_DEV * 2)[:, None]
    group = row // COLS * BLOCK + row % BLOCK
    part = row // BLOCK % (CH_DEV * 2)
    channel = FIRST_CH + group * CH_DEV + part // 2
    phase = (n * channel % NFFT).astype(np.float32) * np.float32(2.0 * math.pi / NFFT)
    phase = phase.astype(np.float64)
    table = np.where(part % 2 == 0, np.cos(phase), -np.sin(phase)).astype(np.float32)
    return (table * np.float32(2.0**-19)).astype(jnp.bfloat16)


def for_each(count, body):
    if count == 1:
        body(0)
    else:
        pl.loop(0, count)(body)


def kernel(
    groups, samples, taps, table, out,
    x_raw, x, taps_v, table_v, weights, prod, volts, turned, send, recv, stack,
    load_sem, sample_sem, send_sem, recv_sem,
):
    me = lax.axis_index("inp")
    blocks = groups // BLOCK
    taps_copy = pltpu.make_async_copy(taps, taps_v, load_sem.at[0])
    table_copy = pltpu.make_async_copy(table, table_v, load_sem.at[1])
    taps_copy.start()
    table_copy.start()
    loads = []
    for index, (first, last) in enumerate(CHUNKS):
        part = pl.ds(first * NFFT, (last - first) * NFFT)
        loads.append(
            pltpu.make_async_copy(samples.at[:, part], x_raw.at[:, part], sample_sem.at[index])
        )
        loads[-1].start()

    barrier = pltpu.get_barrier_semaphore()

    @pl.loop(1, groups)
    def _(step):
        peer = lax.rem(me + step, groups)
        pl.semaphore_signal(
            barrier, inc=1, device_id={"inp": peer}, device_id_type=pl.DeviceIdType.MESH
        )

    taps_copy.wait()
    table_copy.wait()

    def weigh(b):
        values = table_v[pl.ds(b * COLS, COLS), :].astype(jnp.float32)
        for t in range(TAPS):
            tap = taps_v[t : t + 1, :].astype(jnp.float32)
            weights[b, t * COLS : (t + 1) * COLS, :] = (values * tap).astype(jnp.bfloat16)

    for_each(blocks, weigh)

    for index, (first, last) in enumerate(CHUNKS):
        loads[index].wait()
        for f in range(first, last, 2):
            g = min(f + 1, FRAMES - 1)
            x[f * INP_DEV : (f + 2) * INP_DEV, :] = jnp.concatenate(
                [x_raw[:, f * NFFT : (f + 1) * NFFT], x_raw[:, g * NFFT : (g + 1) * NFFT]], axis=0
            )
        rows = slice(first * INP_DEV, (last + last % 2) * INP_DEV)

        def multiply(b):
            prod[b, rows, :] = lax.dot_general(
                x[rows, :], weights[b], (((1,), (1,)), ((), ())), preferred_element_type=jnp.float32
            )

        for_each(blocks, multiply)

    def turn(b):
        count = SPEC * INP_DEV
        half = prod[b, 0 : count + INP_DEV, 0:128] + prod[b, 16 : count + 24, 128:256]
        volts[...] = half[:count] + pltpu.roll(half[INP_DEV:], COLS, 1)
        lane = lax.broadcasted_iota(jnp.int32, (SPEC, 128), 1)
        for i in range(INP_DEV // 2):
            low = volts[pl.ds(i, SPEC, stride=INP_DEV), :]
            high = volts[pl.ds(i + 4, SPEC, stride=INP_DEV), :]
            pair = jnp.where(lane < COLS, low, pltpu.roll(high, COLS, 1)).T
            for k in range(8):
                to = (k % 4) * INP_DEV * BLOCK + (i + 4 * (k // 4)) * BLOCK
                turned[to : to + BLOCK, :] = pair[k * BLOCK : (k + 1) * BLOCK, :]
        for g in range(BLOCK):
            send[b * BLOCK + g] = turned[pl.ds(g, BLOCK_ROWS, stride=BLOCK), :].astype(jnp.bfloat16)

    for_each(blocks, turn)

    pl.semaphore_wait(barrier, groups - 1)

    def transfer(peer):
        return pltpu.make_async_remote_copy(
            src_ref=send.at[peer],
            dst_ref=recv.at[me],
            send_sem=send_sem.at[peer],
            recv_sem=recv_sem.at[me],
            device_id={"inp": peer},
            device_id_type=pl.DeviceIdType.MESH,
        )

    @pl.loop(1, groups)
    def _(step):
        transfer(lax.rem(me + step, groups)).start()

    recv[me] = send[me]

    @pl.loop(1, groups)
    def _(step):
        peer = lax.rem(me + groups - step, groups)
        pltpu.make_async_remote_copy(
            src_ref=send.at[peer],
            dst_ref=recv.at[peer],
            send_sem=send_sem.at[peer],
            recv_sem=recv_sem.at[peer],
            device_id={"inp": peer},
            device_id_type=pl.DeviceIdType.MESH,
        ).wait_recv()

    inputs = groups * INP_DEV
    norm = 1.0 / math.sqrt(SPEC)
    for q in range(CH_DEV):
        for r in range(2):
            at = (2 * q + r) * INP_DEV
            values = recv[:, at : at + INP_DEV, :].astype(jnp.float32).reshape(inputs, SPEC)
            stack[q, 0, :, r * SPEC : (r + 1) * SPEC] = values.astype(jnp.bfloat16)
            turned_part = values if r == 1 else -values
            stack[q, 1, :, (1 - r) * SPEC : (2 - r) * SPEC] = turned_part.astype(jnp.bfloat16)

    def correlate(tile):
        rows = pl.ds(tile * SPEC, SPEC)
        for q in range(CH_DEV):
            for r in range(2):
                product = lax.dot_general(
                    stack[q, r, rows, :], stack[q, 0], (((1,), (1,)), ((), ())),
                    preferred_element_type=jnp.float32,
                )
                out[q, r, rows, :] = (product * norm).astype(jnp.bfloat16)

    for_each(inputs // SPEC, correlate)

    @pl.loop(1, groups)
    def _(step):
        transfer(lax.rem(me + step, groups)).wait_send()


def per_device(samples, taps):
    groups = lax.axis_size("inp")
    blocks = groups // BLOCK
    inputs = groups * INP_DEV
    table = jnp.asarray(dft_table(groups))
    anywhere = pl.BlockSpec(memory_space=pl.ANY)
    bf16, f32 = jnp.bfloat16, jnp.float32
    return pl.pallas_call(
        functools.partial(kernel, groups),
        out_shape=jax.ShapeDtypeStruct((CH_DEV, 2, inputs, inputs), bf16),
        in_specs=[anywhere] * 3,
        out_specs=pl.BlockSpec(memory_space=pltpu.VMEM),
        scratch_shapes=[
            pltpu.VMEM((INP_DEV, FRAMES * NFFT), bf16),
            pltpu.VMEM((PAD_ROWS, NFFT), bf16),
            pltpu.VMEM((TAPS, NFFT), jnp.int32),
            pltpu.VMEM((groups * CH_DEV * 2, NFFT), bf16),
            pltpu.VMEM((blocks, TAPS * COLS, NFFT), bf16),
            pltpu.VMEM((blocks, PAD_ROWS, TAPS * COLS), f32),
            pltpu.VMEM((SPEC * INP_DEV, 128), f32),
            pltpu.VMEM((COLS * INP_DEV, SPEC), f32),
            pltpu.VMEM((groups, BLOCK_ROWS, SPEC), bf16),
            pltpu.VMEM((groups, BLOCK_ROWS, SPEC), bf16),
            pltpu.VMEM((CH_DEV, 2, inputs, 2 * SPEC), bf16),
            pltpu.SemaphoreType.DMA((2,)),
            pltpu.SemaphoreType.DMA((len(CHUNKS),)),
            pltpu.SemaphoreType.DMA((groups,)),
            pltpu.SemaphoreType.DMA((groups,)),
        ],
        compiler_params=pltpu.CompilerParams(
            collective_id=0, has_side_effects=True, vmem_limit_bytes=60 * 2**20
        ),
        name="correlator",
    )(samples, taps, table)


def solution(mesh):
    placed = (P(("band", "inp"), None), P())
    return jax.shard_map(
        per_device,
        mesh=mesh,
        in_specs=placed,
        out_specs=P(("band", "inp"), None, None, None),
        check_vma=False,
    )
```

time: 34.3 us -> 16.2 us (0.47)
  Pallas kernels: 0 us -> 14.5 us
  other arithmetic: 9.34 us -> 0 us
  waiting for transfers between devices: 7.93 us -> 0 us
  starting transfers between devices: 7.39 us -> 0 us
  matrix products: 5.53 us -> 0 us
  local copies, waits for them, and re-layouts: 3.7 us -> 1.57 us
    pallas_call x0 -> x1, Pallas kernels: none -> 14.5 us  [per_device(): pl.pallas_call(functools.partial(kernel, groups), out_shape=jax.ShapeDtyp...]
    convert_element_type x2 -> x0, other arithmetic: 9.29 us -> none  [the longest x1 8.52 us: per_device(): flat_rows = filtered.reshape(per_dev * SPEC, NFFT).astype(jnp.bfloat16)]
    all_to_all x1 -> x0, waiting for transfers between devices: 7.93 us -> none  [per_device(): lax.all_to_all(outgoing, 'inp', split_axis=1, concat_axis=1, tiled=True)]
    all_to_all x1 -> x0, starting transfers between devices: 7.39 us -> none  [per_device(): lax.all_to_all(outgoing, 'inp', split_axis=1, concat_axis=1, tiled=True)]
    dot_general x3 -> x0, matrix products: 5.53 us -> none  [the longest x1 5.13 us: per_device(): lax.dot_general(dft_table, flat_rows, (((0,), (1,)), ((), ())), preferred...]
    convert_element_type x1 -> x0, local copies, waits for them, and re-layouts: 2.3 us -> none  [per_device(): flat_rows = filtered.reshape(per_dev * SPEC, NFFT).astype(jnp.bfloat16)]
    unnamed x3 -> x1, local copies, waits for them, and re-layouts: 0.67 us -> 1.57 us
    reshape x1 -> x0, local copies, waits for them, and re-layouts: 0.66 us -> none  [per_device(): outgoing = voltages.reshape(CH_DEV, groups, 2, per_dev, SPEC)]
  transfers between devices with their start and end apart: 1 -> 0, of which waited for: 1 -> 0; matrix products, arithmetic and copies ran while one was open for 0% -> 0% of each run, Pallas kernels for 0% -> 0%
where the time goes in v1:
time: 16.2 us; the launch traced here: 16.1 us
  Pallas kernels  14.5 us (90%)
  local copies, waits for them, and re-layouts  1.57 us (10%)
    pallas_call x1, Pallas kernels, per_device(): pl.pallas_call(functools.partial(kernel, groups), out_shape=jax.ShapeDtyp...  14.5 us
    unnamed x1, local copies, waits for them, and re-layouts  1.57 us

profile of v1, /device:TPU:0, one launch (start us, length us, event | category | flops | bytes accessed | tf_op | source)
XLA Modules:
  0.0 16.1 jit_solution(2332815668667712186)
XLA Ops:
  0.0 14.5 %correlator.1 = bf16[2,2,128,128]{3,2,1,0:T(8,128)(2,1)} custom-call(bf16[8,268288]{1,0:T(8,128)(2,1)} %samples.1, s32[4,2048]{1,0:T(4,128)} %taps.1, bf16[64,2048]{1,0:T(8,128)(2,1)} %constant.2.clone.table), custom_call_target="tpu_custom_call" | custom-call | tf_op jit(solution)/shard_map/correlator/pallas_call | solution.py:181
  14.5 1.6 %copy.5 = bf16[2,2,128,128]{3,2,1,0:T(8,128)(2,1)} copy(bf16[2,2,128,128]{3,2,1,0:T(8,128)(2,1)} %correlator.1) | data formatting | bytes 262144

commit v2 on v1

--- a/solution.py
+++ b/solution.py
@@ -24,11 +24,11 @@
 
 
 def dft_table(groups):
-    n = np.arange(NFFT, dtype=np.int64)[None, :]
-    row = np.arange(groups * CH_DEV * 2)[:, None]
-    group = row // COLS * BLOCK + row % BLOCK
-    part = row // BLOCK % (CH_DEV * 2)
-    channel = FIRST_CH + group * CH_DEV + part // 2
+    n = np.arange(NFFT, dtype=np.int64)[None, :, None]
+    block = np.arange(groups // BLOCK)[:, None, None]
+    column = np.arange(2 * COLS)[None, None, :] % COLS
+    part = column // BLOCK
+    channel = FIRST_CH + (block * BLOCK + column % BLOCK) * CH_DEV + part // 2
     phase = (n * channel % NFFT).astype(np.float32) * np.float32(2.0 * math.pi / NFFT)
     phase = phase.astype(np.float64)
     table = np.where(part % 2 == 0, np.cos(phase), -np.sin(phase)).astype(np.float32)
@@ -43,8 +43,8 @@
 
 
 def kernel(
-    groups, samples, taps, table, out,
-    x_raw, x, taps_v, table_v, weights, prod, volts, turned, send, recv, stack,
+    groups, samples, taps, table, recv,
+    x_raw, x, taps_v, table_v, weights, prod, volts, turned, send, own_sem,
     load_sem, sample_sem, send_sem, recv_sem,
 ):
     me = lax.axis_index("inp")
@@ -73,11 +73,20 @@
     taps_copy.wait()
     table_copy.wait()
 
+    width = TAPS * COLS
+    tap_rows = taps_v[...].astype(jnp.float32)
+    tap_rows = jnp.concatenate([tap_rows, jnp.zeros_like(tap_rows)], axis=0).astype(jnp.bfloat16)
+    tap_of = lax.broadcasted_iota(jnp.int32, (2 * TAPS, width), 1) // COLS
+    spread = (tap_of == lax.broadcasted_iota(jnp.int32, (2 * TAPS, width), 0)).astype(jnp.bfloat16)
+
     def weigh(b):
-        values = table_v[pl.ds(b * COLS, COLS), :].astype(jnp.float32)
-        for t in range(TAPS):
-            tap = taps_v[t : t + 1, :].astype(jnp.float32)
-            weights[b, t * COLS : (t + 1) * COLS, :] = (values * tap).astype(jnp.bfloat16)
+        spread_taps = lax.dot_general(
+            tap_rows, spread, (((0,), (0,)), ((), ())), preferred_element_type=jnp.float32
+        )
+        values = table_v[b].astype(jnp.float32)
+        for h in range(2):
+            lanes = slice(h * 2 * COLS, (h + 1) * 2 * COLS)
+            weights[b, :, lanes] = (values * spread_taps[:, lanes]).astype(jnp.bfloat16)
 
     for_each(blocks, weigh)
 
@@ -88,11 +97,13 @@
             x[f * INP_DEV : (f + 2) * INP_DEV, :] = jnp.concatenate(
                 [x_raw[:, f * NFFT : (f + 1) * NFFT], x_raw[:, g * NFFT : (g + 1) * NFFT]], axis=0
             )
-        rows = slice(first * INP_DEV, (last + last % 2) * INP_DEV)
+        if index % 2 == 0:
+            continue
+        rows = slice(CHUNKS[index - 1][0] * INP_DEV, (last + last % 2) * INP_DEV)
 
         def multiply(b):
-            prod[b, rows, :] = lax.dot_general(
-                x[rows, :], weights[b], (((1,), (1,)), ((), ())), preferred_element_type=jnp.float32
+            prod[b, rows, :] = jnp.dot(
+                x[rows, :], weights[b], preferred_element_type=jnp.float32
             )
 
         for_each(blocks, multiply)
@@ -130,7 +141,8 @@
     def _(step):
         transfer(lax.rem(me + step, groups)).start()
 
-    recv[me] = send[me]
+    own = pltpu.make_async_copy(send.at[me], recv.at[me], own_sem)
+    own.start()
 
     @pl.loop(1, groups)
     def _(step):
@@ -144,7 +156,15 @@
             device_id_type=pl.DeviceIdType.MESH,
         ).wait_recv()
 
-    inputs = groups * INP_DEV
+    own.wait()
+
+    @pl.loop(1, groups)
+    def _(step):
+        transfer(lax.rem(me + step, groups)).wait_send()
+
+
+def correlate_kernel(recv, out, stack):
+    inputs = recv.shape[0] * INP_DEV
     norm = 1.0 / math.sqrt(SPEC)
     for q in range(CH_DEV):
         for r in range(2):
@@ -166,10 +186,6 @@
 
     for_each(inputs // SPEC, correlate)
 
-    @pl.loop(1, groups)
-    def _(step):
-        transfer(lax.rem(me + step, groups)).wait_send()
-
 
 def per_device(samples, taps):
     groups = lax.axis_size("inp")
@@ -178,23 +194,22 @@
     table = jnp.asarray(dft_table(groups))
     anywhere = pl.BlockSpec(memory_space=pl.ANY)
     bf16, f32 = jnp.bfloat16, jnp.float32
-    return pl.pallas_call(
+    gathered = pl.pallas_call(
         functools.partial(kernel, groups),
-        out_shape=jax.ShapeDtypeStruct((CH_DEV, 2, inputs, inputs), bf16),
+        out_shape=jax.ShapeDtypeStruct((groups, BLOCK_ROWS, SPEC), bf16),
         in_specs=[anywhere] * 3,
-        out_specs=pl.BlockSpec(memory_space=pltpu.VMEM),
+        out_specs=anywhere,
         scratch_shapes=[
             pltpu.VMEM((INP_DEV, FRAMES * NFFT), bf16),
             pltpu.VMEM((PAD_ROWS, NFFT), bf16),
             pltpu.VMEM((TAPS, NFFT), jnp.int32),
-            pltpu.VMEM((groups * CH_DEV * 2, NFFT), bf16),
-            pltpu.VMEM((blocks, TAPS * COLS, NFFT), bf16),
+            pltpu.VMEM((blocks, NFFT, 2 * COLS), bf16),
+            pltpu.VMEM((blocks, NFFT, TAPS * COLS), bf16),
             pltpu.VMEM((blocks, PAD_ROWS, TAPS * COLS), f32),
             pltpu.VMEM((SPEC * INP_DEV, 128), f32),
             pltpu.VMEM((COLS * INP_DEV, SPEC), f32),
             pltpu.VMEM((groups, BLOCK_ROWS, SPEC), bf16),
-            pltpu.VMEM((groups, BLOCK_ROWS, SPEC), bf16),
-            pltpu.VMEM((CH_DEV, 2, inputs, 2 * SPEC), bf16),
+            pltpu.SemaphoreType.DMA,
             pltpu.SemaphoreType.DMA((2,)),
             pltpu.SemaphoreType.DMA((len(CHUNKS),)),
             pltpu.SemaphoreType.DMA((groups,)),
@@ -203,8 +218,17 @@
         compiler_params=pltpu.CompilerParams(
             collective_id=0, has_side_effects=True, vmem_limit_bytes=60 * 2**20
         ),
-        name="correlator",
+        name="channelize",
     )(samples, taps, table)
+    return pl.pallas_call(
+        correlate_kernel,
+        out_shape=jax.ShapeDtypeStruct((CH_DEV, 2, inputs, inputs), bf16),
+        in_specs=[pl.BlockSpec(memory_space=pltpu.VMEM)],
+        out_specs=pl.BlockSpec(memory_space=pltpu.VMEM),
+        scratch_shapes=[pltpu.VMEM((CH_DEV, 2, inputs, 2 * SPEC), bf16)],
+        compiler_params=pltpu.CompilerParams(vmem_limit_bytes=60 * 2**20),
+        name="correlate",
+    )(gathered)
 
 
 def solution(mesh):

time: 16.2 us -> 15.9 us (0.981)
  local copies, waits for them, and re-layouts: 1.57 us -> 0 us
  Pallas kernels: 14.5 us -> 15.8 us
    pallas_call x0 -> x1, Pallas kernels: none -> 1.8 us  [per_device(): pl.pallas_call(correlate_kernel, out_shape=jax.ShapeDtypeStruct((CH_DEV,...]
    unnamed x1 -> x0, local copies, waits for them, and re-layouts: 1.57 us -> none
    pallas_call x1, Pallas kernels: 14.5 us -> 14 us  [per_device(): pl.pallas_call(functools.partial(kernel, groups), out_shape=jax.ShapeDtyp...]
where the time goes in v2:
time: 15.9 us; the launch traced here: 15.8 us
  Pallas kernels  15.8 us (99%)
    pallas_call x1, Pallas kernels, per_device(): pl.pallas_call(functools.partial(kernel, groups), out_shape=jax.ShapeDtyp...  14 us
    pallas_call x1, Pallas kernels, per_device(): pl.pallas_call(correlate_kernel, out_shape=jax.ShapeDtypeStruct((CH_DEV,...  1.8 us

profile of v2, /device:TPU:0, one launch (start us, length us, event | category | flops | bytes accessed | tf_op | source)
XLA Modules:
  0.0 15.8 jit_solution(10244253456605271001)
XLA Ops:
  0.0 14.0 %channelize.1.recv = bf16[16,32,128]{2,1,0:T(8,128)(2,1)} custom-call(bf16[8,268288]{1,0:T(8,128)(2,1)} %samples.1, s32[4,2048]{1,0:T(4,128)} %taps.1, bf16[1,2048,128]{2,1,0:T(8,128)(2,1)} %constant.2.clone.table), custom_call_target="tpu_custom_call" | custom-call | tf_op jit(solution)/shard_map/channelize/pallas_call | solution.py:197
  14.0 1.8 %correlate.1 = bf16[2,2,128,128]{3,2,1,0:T(8,128)(2,1)} custom-call(bf16[16,32,128]{2,1,0:T(8,128)(2,1)} %channelize.1.recv), custom_call_target="tpu_custom_call" | custom-call | tf_op jit(solution)/shard_map/correlate/pallas_call | solution.py:223

commit v3 on v2

v3 whole, which is shorter than its diff:
```python
import functools
import math

import jax
import jax.numpy as jnp
import numpy as np
from jax import lax
from jax.experimental import pallas as pl
from jax.experimental.pallas import tpu as pltpu
from jax.sharding import PartitionSpec as P

CH_DEV = 2
NFFT = 2048
TAPS = 4
FIRST_CH = 256
SPEC = 128
INP_DEV = 8
FRAMES = SPEC + TAPS - 1
BLOCK = 16
COLS = BLOCK * CH_DEV * 2
HALF = SPEC // 2
HALF_FRAMES = 68
HALF_ROWS = HALF_FRAMES * INP_DEV
LATE_FRAMES = FRAMES - HALF_FRAMES
LOADS = ((0, 32), (32, LATE_FRAMES - 32))
BLOCK_ROWS = CH_DEV * INP_DEV


def dft_table(groups):
    n = np.arange(NFFT, dtype=np.int64)[None, :, None]
    block = np.arange(groups // BLOCK)[:, None, None]
    column = np.arange(2 * COLS)[None, None, :] % COLS
    part = column // BLOCK
    channel = FIRST_CH + (block * BLOCK + column % BLOCK) * CH_DEV + part % CH_DEV
    phase = (n * channel % NFFT).astype(np.float32) * np.float32(2.0 * math.pi / NFFT)
    phase = phase.astype(np.float64)
    table = np.where(part < CH_DEV, np.cos(phase), -np.sin(phase)).astype(np.float32)
    return (table * np.float32(2.0**-19)).astype(jnp.bfloat16)


def for_each(count, body):
    if count == 1:
        body(0)
    else:
        pl.loop(0, count)(body)


def kernel(
    groups, samples, taps, table, recv,
    x_raw, x, taps_v, table_v, weights, prod, volts, turned, send,
    load_sem, sample_sem, own_sem, send_sem, recv_sem,
):
    me = lax.axis_index("inp")
    blocks = groups // BLOCK
    taps_copy = pltpu.make_async_copy(taps, taps_v, load_sem.at[0])
    table_copy = pltpu.make_async_copy(table, table_v, load_sem.at[1])
    taps_copy.start()
    table_copy.start()

    def load(first, count, sem):
        part = pl.ds(first * NFFT, count * NFFT)
        return pltpu.make_async_copy(samples.at[:, part], x_raw.at[:, part], sem)

    extra = load(LATE_FRAMES, HALF_FRAMES - LATE_FRAMES, load_sem.at[2])
    for h in range(2):
        for index, (first, count) in enumerate(LOADS):
            load(h * HALF_FRAMES + first, count, sample_sem.at[h, index]).start()
        if h == 0:
            extra.start()

    barrier = pltpu.get_barrier_semaphore()

    @pl.loop(1, groups)
    def _(step):
        peer = lax.rem(me + step, groups)
        pl.semaphore_signal(
            barrier, inc=1, device_id={"inp": peer}, device_id_type=pl.DeviceIdType.MESH
        )

    width = TAPS * COLS
    tap_of = lax.broadcasted_iota(jnp.int32, (2 * TAPS, width), 1) // COLS
    spread = (tap_of == lax.broadcasted_iota(jnp.int32, (2 * TAPS, width), 0)).astype(jnp.bfloat16)
    taps_copy.wait()
    table_copy.wait()

    @pl.loop(0, NFFT // 512)
    def _(tile):
        rows = pl.ds(pl.multiple_of(tile * 512, 512), 512)
        tap_rows = taps_v[:, rows].astype(jnp.float32)
        tap_rows = jnp.concatenate([tap_rows, jnp.zeros_like(tap_rows)], axis=0)
        spread_taps = lax.dot_general(
            tap_rows.astype(jnp.bfloat16), spread, (((0,), (0,)), ((), ())),
            preferred_element_type=jnp.float32,
        )

        def weigh(b):
            values = table_v[b, rows, :].astype(jnp.float32)
            for h in range(2):
                lanes = slice(h * 2 * COLS, (h + 1) * 2 * COLS)
                weights[b, rows, lanes] = (values * spread_taps[:, lanes]).astype(jnp.bfloat16)

        for_each(blocks, weigh)

    extra.wait()

    def transfer(peer, slot, h):
        return pltpu.make_async_remote_copy(
            src_ref=send.at[peer, h],
            dst_ref=recv.at[slot, h],
            send_sem=send_sem.at[h, peer],
            recv_sem=recv_sem.at[h, slot],
            device_id={"inp": peer},
            device_id_type=pl.DeviceIdType.MESH,
        )

    def own(h):
        return pltpu.make_async_copy(send.at[me, h], recv.at[me, h], own_sem.at[h])

    @pl.loop(0, 2)
    def _(h):
        for index, (first, count) in enumerate(LOADS):
            load(h * HALF_FRAMES + first, count, sample_sem.at[h, index]).wait()

        @pl.loop(0, HALF_FRAMES // 4)
        def _(quad):
            for pair in range(2):
                f = quad * 4 + pair * 2
                frames = [
                    x_raw[:, pl.ds(pl.multiple_of((h * HALF_FRAMES + f + k) * NFFT, NFFT), NFFT)]
                    for k in range(2)
                ]
                rows = pl.ds(pl.multiple_of(f * INP_DEV, 16), 16)
                x[rows, :] = jnp.concatenate(frames, axis=0)

        def multiply(b):
            rows = pl.ds(pl.multiple_of(h * HALF_ROWS, HALF_ROWS), HALF_ROWS)
            prod[b, rows, :] = jnp.dot(x[...], weights[b], preferred_element_type=jnp.float32)

        for_each(blocks, multiply)

        def turn(b):
            count = HALF * INP_DEV
            start = pl.multiple_of(h * count, count)
            half = (
                prod[b, pl.ds(start, count + INP_DEV), 0:128]
                + prod[b, pl.ds(start + 2 * INP_DEV, count + INP_DEV), 128:256]
            )
            volts[...] = half[:count] + pltpu.roll(half[INP_DEV:], COLS, 1)
            low_lanes = lax.broadcasted_iota(jnp.int32, (HALF, 128), 1) < COLS
            for p in range(2):
                rows = []
                for ia in range(2):
                    i = 4 * ia + 2 * p
                    low = volts[pl.ds(i, HALF, stride=INP_DEV), :]
                    high = volts[pl.ds(i + 1, HALF, stride=INP_DEV), :]
                    rows.append(jnp.where(low_lanes, low, pltpu.roll(high, COLS, 1)))
                pair = jnp.concatenate(rows, axis=0).T
                for k in range(8):
                    to = ((k % 4) * 4 + 2 * p + k // 4) * BLOCK
                    turned[to : to + BLOCK, :] = pair[k * BLOCK : (k + 1) * BLOCK, :]
            first = lax.broadcasted_iota(jnp.int32, (INP_DEV, 128), 1) < HALF
            for g in range(BLOCK):
                real = turned[pl.ds(g, 8, stride=BLOCK), :]
                imag = turned[pl.ds(8 * BLOCK + g, 8, stride=BLOCK), :]
                send[b * BLOCK + g, h] = jnp.concatenate(
                    [
                        jnp.where(first, real, pltpu.roll(imag, HALF, 1)),
                        jnp.where(first, pltpu.roll(real, HALF, 1), imag),
                    ],
                    axis=0,
                ).astype(jnp.bfloat16)

        for_each(blocks, turn)

        @pl.when(h == 0)
        def _():
            pl.semaphore_wait(barrier, groups - 1)

        @pl.loop(1, groups)
        def _(step):
            transfer(lax.rem(me + step, groups), me, h).start()

        own(h).start()

    for h in range(2):

        @pl.loop(1, groups)
        def _(step):
            peer = lax.rem(me + groups - step, groups)
            transfer(peer, peer, h).wait_recv()

    for h in range(2):
        own(h).wait()

        @pl.loop(1, groups)
        def _(step):
            transfer(lax.rem(me + step, groups), me, h).wait_send()


def correlate_kernel(recv, out, stack):
    inputs = recv.shape[0] * INP_DEV
    norm = 1.0 / math.sqrt(SPEC)
    shape = (recv.shape[0], INP_DEV, 128)
    upper = lax.broadcasted_iota(jnp.int32, shape, 1) < 4
    first = lax.broadcasted_iota(jnp.int32, (inputs, 128), 1) < HALF
    for h in range(2):
        lanes = slice(h * 128, (h + 1) * 128)
        early = recv[:, h, 0:INP_DEV, :].astype(jnp.float32)
        late = recv[:, h, INP_DEV:, :].astype(jnp.float32)
        by_channel = (
            jnp.where(upper, early, pltpu.roll(late, 4, 1)),
            jnp.where(upper, pltpu.roll(early, 4, 1), late),
        )
        for q in range(CH_DEV):
            values = by_channel[q].reshape(inputs, 128)
            rolled = pltpu.roll(values, HALF, 1)
            stack[q, 0, :, lanes] = values.astype(jnp.bfloat16)
            stack[q, 1, :, lanes] = jnp.where(first, rolled, -rolled).astype(jnp.bfloat16)

    def correlate(tile):
        rows = pl.ds(tile * 128, 128)
        for q in range(CH_DEV):
            for r in range(2):
                product = lax.dot_general(
                    stack[q, r, rows, :], stack[q, 0], (((1,), (1,)), ((), ())),
                    preferred_element_type=jnp.float32,
                )
                out[q, r, rows, :] = (product * norm).astype(jnp.bfloat16)

    for_each(inputs // 128, correlate)


def per_device(samples, taps):
    groups = lax.axis_size("inp")
    blocks = groups // BLOCK
    inputs = groups * INP_DEV
    table = jnp.asarray(dft_table(groups))
    anywhere = pl.BlockSpec(memory_space=pl.ANY)
    bf16, f32 = jnp.bfloat16, jnp.float32
    gathered = pl.pallas_call(
        functools.partial(kernel, groups),
        out_shape=jax.ShapeDtypeStruct((groups, 2, BLOCK_ROWS, 128), bf16),
        in_specs=[anywhere] * 3,
        out_specs=anywhere,
        scratch_shapes=[
            pltpu.VMEM((INP_DEV, 2 * HALF_FRAMES * NFFT), bf16),
            pltpu.VMEM((HALF_ROWS, NFFT), bf16),
            pltpu.VMEM((TAPS, NFFT), jnp.int32),
            pltpu.VMEM((blocks, NFFT, 2 * COLS), bf16),
            pltpu.VMEM((blocks, NFFT, TAPS * COLS), bf16),
            pltpu.VMEM((blocks, 2 * HALF_ROWS, TAPS * COLS), f32),
            pltpu.VMEM((HALF * INP_DEV, 128), f32),
            pltpu.VMEM((BLOCK_ROWS * BLOCK, 128), f32),
            pltpu.VMEM((groups, 2, BLOCK_ROWS, 128), bf16),
            pltpu.SemaphoreType.DMA((3,)),
            pltpu.SemaphoreType.DMA((2, len(LOADS))),
            pltpu.SemaphoreType.DMA((2,)),
            pltpu.SemaphoreType.DMA((2, groups)),
            pltpu.SemaphoreType.DMA((2, groups)),
        ],
        compiler_params=pltpu.CompilerParams(
            collective_id=0, has_side_effects=True, vmem_limit_bytes=60 * 2**20
        ),
        name="channelize",
    )(samples, taps, table)
    return pl.pallas_call(
        correlate_kernel,
        out_shape=jax.ShapeDtypeStruct((CH_DEV, 2, inputs, inputs), bf16),
        in_specs=[pl.BlockSpec(memory_space=pltpu.VMEM)],
        out_specs=pl.BlockSpec(memory_space=pltpu.VMEM),
        scratch_shapes=[pltpu.VMEM((CH_DEV, 2, inputs, 2 * SPEC), bf16)],
        compiler_params=pltpu.CompilerParams(vmem_limit_bytes=60 * 2**20),
        name="correlate",
    )(gathered)


def solution(mesh):
    placed = (P(("band", "inp"), None), P())
    return jax.shard_map(
        per_device,
        mesh=mesh,
        in_specs=placed,
        out_specs=P(("band", "inp"), None, None, None),
        check_vma=False,
    )
```

time: 15.9 us -> 16.6 us (1.044)
  Pallas kernels: 15.8 us -> 16.5 us
    pallas_call x1, Pallas kernels: 14 us -> 14.6 us  [per_device(): pl.pallas_call(functools.partial(kernel, groups), out_shape=jax.ShapeDtyp...]
where the time goes in v3:
time: 16.6 us; the launch traced here: 16.5 us
  Pallas kernels  16.5 us (99%)
    pallas_call x1, Pallas kernels, per_device(): pl.pallas_call(functools.partial(kernel, groups), out_shape=jax.ShapeDtyp...  14.6 us
    pallas_call x1, Pallas kernels, per_device(): pl.pallas_call(correlate_kernel, out_shape=jax.ShapeDtypeStruct((CH_DEV,...  1.84 us

profile of v3, /device:TPU:0, one launch (start us, length us, event | category | flops | bytes accessed | tf_op | source)
XLA Modules:
  0.0 16.5 jit_solution(18434054127443264623)
XLA Ops:
  0.0 14.6 %channelize.1.recv = bf16[16,2,16,128]{3,2,1,0:T(8,128)(2,1)} custom-call(bf16[8,268288]{1,0:T(8,128)(2,1)} %samples.1, s32[4,2048]{1,0:T(4,128)} %taps.1, bf16[1,2048,128]{2,1,0:T(8,128)(2,1)} %constant.2.clone.table), custom_call_target="tpu_custom_call" | custom-call | tf_op jit(solution)/shard_map/channelize/pallas_call | solution.py:240
  14.7 1.8 %correlate.1 = bf16[2,2,128,128]{3,2,1,0:T(8,128)(2,1)} custom-call(bf16[16,2,16,128]{3,2,1,0:T(8,128)(2,1)} %channelize.1.recv), custom_call_target="tpu_custom_call" | custom-call | tf_op jit(solution)/shard_map/correlate/pallas_call | solution.py:266

commit v4 on v3

--- a/solution.py
+++ b/solution.py
@@ -45,6 +45,14 @@
         pl.loop(0, count)(body)
 
 
+def for_each_peer(groups, body):
+    if groups <= BLOCK:
+        for step in range(1, groups):
+            body(step)
+    else:
+        pl.loop(1, groups)(body)
+
+
 def kernel(
     groups, samples, taps, table, recv,
     x_raw, x, taps_v, table_v, weights, prod, volts, turned, send,
@@ -70,12 +78,13 @@
 
     barrier = pltpu.get_barrier_semaphore()
 
-    @pl.loop(1, groups)
-    def _(step):
+    def greet(step):
         peer = lax.rem(me + step, groups)
         pl.semaphore_signal(
             barrier, inc=1, device_id={"inp": peer}, device_id_type=pl.DeviceIdType.MESH
         )
+
+    for_each_peer(groups, greet)
 
     width = TAPS * COLS
     tap_of = lax.broadcasted_iota(jnp.int32, (2 * TAPS, width), 1) // COLS
@@ -83,32 +92,28 @@
     taps_copy.wait()
     table_copy.wait()
 
-    @pl.loop(0, NFFT // 512)
-    def _(tile):
-        rows = pl.ds(pl.multiple_of(tile * 512, 512), 512)
-        tap_rows = taps_v[:, rows].astype(jnp.float32)
-        tap_rows = jnp.concatenate([tap_rows, jnp.zeros_like(tap_rows)], axis=0)
-        spread_taps = lax.dot_general(
-            tap_rows.astype(jnp.bfloat16), spread, (((0,), (0,)), ((), ())),
-            preferred_element_type=jnp.float32,
-        )
-
-        def weigh(b):
-            values = table_v[b, rows, :].astype(jnp.float32)
-            for h in range(2):
-                lanes = slice(h * 2 * COLS, (h + 1) * 2 * COLS)
-                weights[b, rows, lanes] = (values * spread_taps[:, lanes]).astype(jnp.bfloat16)
-
-        for_each(blocks, weigh)
+    tap_rows = taps_v[...].astype(jnp.float32)
+    tap_rows = jnp.concatenate([tap_rows, jnp.zeros_like(tap_rows)], axis=0).astype(jnp.bfloat16)
+    spread_taps = lax.dot_general(
+        tap_rows, spread, (((0,), (0,)), ((), ())), preferred_element_type=jnp.float32
+    )
+
+    def weigh(b):
+        values = table_v[b].astype(jnp.float32)
+        for h in range(2):
+            lanes = slice(h * 2 * COLS, (h + 1) * 2 * COLS)
+            weights[b, :, lanes] = (values * spread_taps[:, lanes]).astype(jnp.bfloat16)
+
+    for_each(blocks, weigh)
 
     extra.wait()
 
-    def transfer(peer, slot, h):
+    def transfer(peer, source, target):
         return pltpu.make_async_remote_copy(
-            src_ref=send.at[peer, h],
-            dst_ref=recv.at[slot, h],
-            send_sem=send_sem.at[h, peer],
-            recv_sem=recv_sem.at[h, slot],
+            src_ref=source,
+            dst_ref=target,
+            send_sem=send_sem,
+            recv_sem=recv_sem,
             device_id={"inp": peer},
             device_id_type=pl.DeviceIdType.MESH,
         )
@@ -121,16 +126,15 @@
         for index, (first, count) in enumerate(LOADS):
             load(h * HALF_FRAMES + first, count, sample_sem.at[h, index]).wait()
 
-        @pl.loop(0, HALF_FRAMES // 4)
-        def _(quad):
-            for pair in range(2):
-                f = quad * 4 + pair * 2
-                frames = [
-                    x_raw[:, pl.ds(pl.multiple_of((h * HALF_FRAMES + f + k) * NFFT, NFFT), NFFT)]
-                    for k in range(2)
-                ]
-                rows = pl.ds(pl.multiple_of(f * INP_DEV, 16), 16)
-                x[rows, :] = jnp.concatenate(frames, axis=0)
+        for column in range(0, NFFT, 256):
+            for f in range(0, HALF_FRAMES, 2):
+                frames = []
+                for k in range(2):
+                    start = pl.multiple_of((h * HALF_FRAMES + f + k) * NFFT + column, 256)
+                    frames.append(x_raw[:, pl.ds(start, 256)])
+                x[f * INP_DEV : (f + 2) * INP_DEV, column : column + 256] = jnp.concatenate(
+                    frames, axis=0
+                )
 
         def multiply(b):
             rows = pl.ds(pl.multiple_of(h * HALF_ROWS, HALF_ROWS), HALF_ROWS)
@@ -176,25 +180,20 @@
         def _():
             pl.semaphore_wait(barrier, groups - 1)
 
-        @pl.loop(1, groups)
-        def _(step):
-            transfer(lax.rem(me + step, groups), me, h).start()
+        def start(step):
+            peer = lax.rem(me + step, groups)
+            transfer(peer, send.at[peer, h], recv.at[me, h]).start()
+
+        for_each_peer(groups, start)
 
         own(h).start()
-
-    for h in range(2):
-
-        @pl.loop(1, groups)
-        def _(step):
-            peer = lax.rem(me + groups - step, groups)
-            transfer(peer, peer, h).wait_recv()
 
     for h in range(2):
         own(h).wait()
-
-        @pl.loop(1, groups)
-        def _(step):
-            transfer(lax.rem(me + step, groups), me, h).wait_send()
+    others = pl.ds(0, groups - 1)
+    everything = transfer(lax.rem(me + 1, groups), send.at[others], recv.at[others])
+    everything.wait_recv()
+    everything.wait_send()
 
 
 def correlate_kernel(recv, out, stack):
@@ -239,9 +238,9 @@
     bf16, f32 = jnp.bfloat16, jnp.float32
     gathered = pl.pallas_call(
         functools.partial(kernel, groups),
-        out_shape=jax.ShapeDtypeStruct((groups, 2, BLOCK_ROWS, 128), bf16),
-        in_specs=[anywhere] * 3,
-        out_specs=anywhere,
+        out_shape=pltpu.VMEM((groups, 2, BLOCK_ROWS, 128), bf16),
+        in_specs=[pl.BlockSpec(memory_space=pltpu.HBM)] * 3,
+        out_specs=pl.BlockSpec(memory_space=pltpu.VMEM),
         scratch_shapes=[
             pltpu.VMEM((INP_DEV, 2 * HALF_FRAMES * NFFT), bf16),
             pltpu.VMEM((HALF_ROWS, NFFT), bf16),
@@ -255,11 +254,11 @@
             pltpu.SemaphoreType.DMA((3,)),
             pltpu.SemaphoreType.DMA((2, len(LOADS))),
             pltpu.SemaphoreType.DMA((2,)),
-            pltpu.SemaphoreType.DMA((2, groups)),
-            pltpu.SemaphoreType.DMA((2, groups)),
+            pltpu.SemaphoreType.DMA,
+            pltpu.SemaphoreType.DMA,
         ],
         compiler_params=pltpu.CompilerParams(
-            collective_id=0, has_side_effects=True, vmem_limit_bytes=60 * 2**20
+            collective_id=0, has_side_effects=True, vmem_limit_bytes=58 * 2**20
         ),
         name="channelize",
     )(samples, taps, table)
@@ -269,7 +268,7 @@
         in_specs=[pl.BlockSpec(memory_space=pltpu.VMEM)],
         out_specs=pl.BlockSpec(memory_space=pltpu.VMEM),
         scratch_shapes=[pltpu.VMEM((CH_DEV, 2, inputs, 2 * SPEC), bf16)],
-        compiler_params=pltpu.CompilerParams(vmem_limit_bytes=60 * 2**20),
+        compiler_params=pltpu.CompilerParams(vmem_limit_bytes=2**20 * (4 + groups // 4)),
         name="correlate",
     )(gathered)
 

time: 16.6 us -> 13.2 us (0.80)
  Pallas kernels: 16.5 us -> 13.1 us
    pallas_call x1, Pallas kernels: 14.6 us -> 12.1 us  [per_device(): pl.pallas_call(functools.partial(kernel, groups), out_shape=pltpu.VMEM((g...]
    pallas_call x1, Pallas kernels: 1.84 us -> 0.94 us  [per_device(): pl.pallas_call(correlate_kernel, out_shape=jax.ShapeDtypeStruct((CH_DEV,...]
where the time goes in v4:
time: 13.2 us; the launch traced here: 13.1 us
  Pallas kernels  13.1 us (99%)
    pallas_call x1, Pallas kernels, per_device(): pl.pallas_call(functools.partial(kernel, groups), out_shape=pltpu.VMEM((g...  12.1 us
    pallas_call x1, Pallas kernels, per_device(): pl.pallas_call(correlate_kernel, out_shape=jax.ShapeDtypeStruct((CH_DEV,...  0.94 us

profile of v4, /device:TPU:0, one launch (start us, length us, event | category | flops | bytes accessed | tf_op | source)
XLA Modules:
  0.0 13.1 jit_solution(13721193723618457703)
XLA Ops:
  0.0 12.1 %channelize.1.recv = bf16[16,2,16,128]{3,2,1,0:T(8,128)(2,1)S(1)} custom-call(bf16[8,268288]{1,0:T(8,128)(2,1)} %samples.1, s32[4,2048]{1,0:T(4,128)} %taps.1, bf16[1,2048,128]{2,1,0:T(8,128)(2,1)} %constant.2.clone.table), custom_call_target="tpu_custom_call" | custom-call | tf_op jit(solution)/shard_map/channelize/pallas_call | solution.py:239
  12.1 0.9 %correlate.1 = bf16[2,2,128,128]{3,2,1,0:T(8,128)(2,1)} custom-call(bf16[16,2,16,128]{3,2,1,0:T(8,128)(2,1)S(1)} %channelize.1.recv), custom_call_target="tpu_custom_call" | custom-call | tf_op jit(solution)/shard_map/correlate/pallas_call | solution.py:265

commit v5 on v4

--- a/solution.py
+++ b/solution.py
@@ -55,7 +55,7 @@
 
 def kernel(
     groups, samples, taps, table, recv,
-    x_raw, x, taps_v, table_v, weights, prod, volts, turned, send,
+    x, taps_v, table_v, weights, prod, volts, turned, send,
     load_sem, sample_sem, own_sem, send_sem, recv_sem,
 ):
     me = lax.axis_index("inp")
@@ -66,8 +66,8 @@
     table_copy.start()
 
     def load(first, count, sem):
-        part = pl.ds(first * NFFT, count * NFFT)
-        return pltpu.make_async_copy(samples.at[:, part], x_raw.at[:, part], sem)
+        part = pl.ds(first, count)
+        return pltpu.make_async_copy(samples.at[part], x.at[part], sem)
 
     extra = load(LATE_FRAMES, HALF_FRAMES - LATE_FRAMES, load_sem.at[2])
     for h in range(2):
@@ -126,19 +126,10 @@
         for index, (first, count) in enumerate(LOADS):
             load(h * HALF_FRAMES + first, count, sample_sem.at[h, index]).wait()
 
-        for column in range(0, NFFT, 256):
-            for f in range(0, HALF_FRAMES, 2):
-                frames = []
-                for k in range(2):
-                    start = pl.multiple_of((h * HALF_FRAMES + f + k) * NFFT + column, 256)
-                    frames.append(x_raw[:, pl.ds(start, 256)])
-                x[f * INP_DEV : (f + 2) * INP_DEV, column : column + 256] = jnp.concatenate(
-                    frames, axis=0
-                )
-
         def multiply(b):
             rows = pl.ds(pl.multiple_of(h * HALF_ROWS, HALF_ROWS), HALF_ROWS)
-            prod[b, rows, :] = jnp.dot(x[...], weights[b], preferred_element_type=jnp.float32)
+            values = x[pl.ds(h * HALF_FRAMES, HALF_FRAMES)].reshape(HALF_ROWS, NFFT)
+            prod[b, rows, :] = jnp.dot(values, weights[b], preferred_element_type=jnp.float32)
 
         for_each(blocks, multiply)
 
@@ -234,6 +225,7 @@
     blocks = groups // BLOCK
     inputs = groups * INP_DEV
     table = jnp.asarray(dft_table(groups))
+    frames = samples.reshape(INP_DEV, FRAMES, NFFT).transpose(1, 0, 2)
     anywhere = pl.BlockSpec(memory_space=pl.ANY)
     bf16, f32 = jnp.bfloat16, jnp.float32
     gathered = pl.pallas_call(
@@ -242,8 +234,7 @@
         in_specs=[pl.BlockSpec(memory_space=pltpu.HBM)] * 3,
         out_specs=pl.BlockSpec(memory_space=pltpu.VMEM),
         scratch_shapes=[
-            pltpu.VMEM((INP_DEV, 2 * HALF_FRAMES * NFFT), bf16),
-            pltpu.VMEM((HALF_ROWS, NFFT), bf16),
+            pltpu.VMEM((2 * HALF_FRAMES, INP_DEV, NFFT), bf16),
             pltpu.VMEM((TAPS, NFFT), jnp.int32),
             pltpu.VMEM((blocks, NFFT, 2 * COLS), bf16),
             pltpu.VMEM((blocks, NFFT, TAPS * COLS), bf16),
@@ -261,7 +252,7 @@
             collective_id=0, has_side_effects=True, vmem_limit_bytes=58 * 2**20
         ),
         name="channelize",
-    )(samples, taps, table)
+    )(frames, taps, table)
     return pl.pallas_call(
         correlate_kernel,
         out_shape=jax.ShapeDtypeStruct((CH_DEV, 2, inputs, inputs), bf16),

time: 13.2 us -> 13.1 us (level)
  no operation moved by 1% of the time
where the time goes in v5:
time: 13.1 us; the launch traced here: 13 us
  Pallas kernels  13 us (99%)
    pallas_call x1, Pallas kernels, per_device(): pl.pallas_call(functools.partial(kernel, groups), out_shape=pltpu.VMEM((g...  12.1 us
    pallas_call x1, Pallas kernels, per_device(): pl.pallas_call(correlate_kernel, out_shape=jax.ShapeDtypeStruct((CH_DEV,...  0.94 us

profile of v5, /device:TPU:0, one launch (start us, length us, event | category | flops | bytes accessed | tf_op | source)
XLA Modules:
  0.0 13.0 jit_solution(8689924780253896379)
XLA Ops:
  0.0 12.1 %channelize.1.recv = bf16[16,2,16,128]{3,2,1,0:T(8,128)(2,1)S(1)} custom-call(bf16[131,8,2048]{2,1,0:T(8,128)(2,1)} %bitcast.3, s32[4,2048]{1,0:T(4,128)} %taps.1, bf16[1,2048,128]{2,1,0:T(8,128)(2,1)} %constant.2.clone.table), custom_call_target="tpu_custom_call" | custom-call | tf_op jit(solution)/shard_map/channelize/pallas_call | solution.py:231
  12.1 0.9 %correlate.1 = bf16[2,2,128,128]{3,2,1,0:T(8,128)(2,1)} custom-call(bf16[16,2,16,128]{3,2,1,0:T(8,128)(2,1)S(1)} %channelize.1.recv), custom_call_target="tpu_custom_call" | custom-call | tf_op jit(solution)/shard_map/correlate/pallas_call | solution.py:256

commit v6 on v5

--- a/solution.py
+++ b/solution.py
@@ -121,21 +121,21 @@
     def own(h):
         return pltpu.make_async_copy(send.at[me, h], recv.at[me, h], own_sem.at[h])
 
-    @pl.loop(0, 2)
-    def _(h):
+    def multiply_half(h):
         for index, (first, count) in enumerate(LOADS):
             load(h * HALF_FRAMES + first, count, sample_sem.at[h, index]).wait()
 
         def multiply(b):
-            rows = pl.ds(pl.multiple_of(h * HALF_ROWS, HALF_ROWS), HALF_ROWS)
+            rows = pl.ds(h * HALF_ROWS, HALF_ROWS)
             values = x[pl.ds(h * HALF_FRAMES, HALF_FRAMES)].reshape(HALF_ROWS, NFFT)
             prod[b, rows, :] = jnp.dot(values, weights[b], preferred_element_type=jnp.float32)
 
         for_each(blocks, multiply)
 
+    def turn_half(h):
         def turn(b):
             count = HALF * INP_DEV
-            start = pl.multiple_of(h * count, count)
+            start = h * count
             half = (
                 prod[b, pl.ds(start, count + INP_DEV), 0:128]
                 + prod[b, pl.ds(start + 2 * INP_DEV, count + INP_DEV), 128:256]
@@ -167,17 +167,21 @@
 
         for_each(blocks, turn)
 
-        @pl.when(h == 0)
-        def _():
-            pl.semaphore_wait(barrier, groups - 1)
-
+    def send_half(h):
         def start(step):
             peer = lax.rem(me + step, groups)
             transfer(peer, send.at[peer, h], recv.at[me, h]).start()
 
         for_each_peer(groups, start)
-
         own(h).start()
+
+    multiply_half(0)
+    multiply_half(1)
+    turn_half(0)
+    pl.semaphore_wait(barrier, groups - 1)
+    send_half(0)
+    turn_half(1)
+    send_half(1)
 
     for h in range(2):
         own(h).wait()
@@ -187,7 +191,7 @@
     everything.wait_send()
 
 
-def correlate_kernel(recv, out, stack):
+def correlate_kernel(recv, out, stack, result, out_sem):
     inputs = recv.shape[0] * INP_DEV
     norm = 1.0 / math.sqrt(SPEC)
     shape = (recv.shape[0], INP_DEV, 128)
@@ -207,17 +211,22 @@
             stack[q, 0, :, lanes] = values.astype(jnp.bfloat16)
             stack[q, 1, :, lanes] = jnp.where(first, rolled, -rolled).astype(jnp.bfloat16)
 
-    def correlate(tile):
-        rows = pl.ds(tile * 128, 128)
-        for q in range(CH_DEV):
-            for r in range(2):
-                product = lax.dot_general(
-                    stack[q, r, rows, :], stack[q, 0], (((1,), (1,)), ((), ())),
-                    preferred_element_type=jnp.float32,
-                )
-                out[q, r, rows, :] = (product * norm).astype(jnp.bfloat16)
-
-    for_each(inputs // 128, correlate)
+    for q in range(CH_DEV):
+
+        def correlate(tile):
+            rows = pl.ds(tile * 128, 128)
+            left = jnp.concatenate([stack[q, 0, rows, :], stack[q, 1, rows, :]], axis=0)
+            product = lax.dot_general(
+                left, stack[q, 0], (((1,), (1,)), ((), ())), preferred_element_type=jnp.float32
+            )
+            product = (product * norm).astype(jnp.bfloat16)
+            result[q, 0, rows, :] = product[:128]
+            result[q, 1, rows, :] = product[128:]
+
+        for_each(inputs // 128, correlate)
+        pltpu.make_async_copy(result.at[q], out.at[q], out_sem.at[q]).start()
+    for q in range(CH_DEV):
+        pltpu.make_async_copy(result.at[q], out.at[q], out_sem.at[q]).wait()
 
 
 def per_device(samples, taps):
@@ -257,8 +266,12 @@
         correlate_kernel,
         out_shape=jax.ShapeDtypeStruct((CH_DEV, 2, inputs, inputs), bf16),
         in_specs=[pl.BlockSpec(memory_space=pltpu.VMEM)],
-        out_specs=pl.BlockSpec(memory_space=pltpu.VMEM),
-        scratch_shapes=[pltpu.VMEM((CH_DEV, 2, inputs, 2 * SPEC), bf16)],
+        out_specs=anywhere,
+        scratch_shapes=[
+            pltpu.VMEM((CH_DEV, 2, inputs, 2 * SPEC), bf16),
+            pltpu.VMEM((CH_DEV, 2, inputs, inputs), bf16),
+            pltpu.SemaphoreType.DMA((CH_DEV,)),
+        ],
         compiler_params=pltpu.CompilerParams(vmem_limit_bytes=2**20 * (4 + groups // 4)),
         name="correlate",
     )(gathered)

time: 13.1 us -> 14 us (1.069)
  Pallas kernels: 13 us -> 13.8 us
    pallas_call x1, Pallas kernels: 12.1 us -> 12.9 us  [per_device(): pl.pallas_call(functools.partial(kernel, groups), out_shape=pltpu.VMEM((g...]
where the time goes in v6:
time: 14 us; the launch traced here: 13.8 us
  Pallas kernels  13.8 us (99%)
    pallas_call x1, Pallas kernels, per_device(): pl.pallas_call(functools.partial(kernel, groups), out_shape=pltpu.VMEM((g...  12.9 us
    pallas_call x1, Pallas kernels, per_device(): pl.pallas_call(correlate_kernel, out_shape=jax.ShapeDtypeStruct((CH_DEV,...  0.95 us

profile of v6, /device:TPU:0, one launch (start us, length us, event | category | flops | bytes accessed | tf_op | source)
XLA Modules:
  0.0 13.8 jit_solution(7321671738058679287)
XLA Ops:
  0.0 12.9 %channelize.1.recv = bf16[16,2,16,128]{3,2,1,0:T(8,128)(2,1)S(1)} custom-call(bf16[131,8,2048]{2,1,0:T(8,128)(2,1)} %bitcast.3, s32[4,2048]{1,0:T(4,128)} %taps.1, bf16[1,2048,128]{2,1,0:T(8,128)(2,1)} %constant.2.clone.table), custom_call_target="tpu_custom_call" | custom-call | tf_op jit(solution)/shard_map/channelize/pallas_call | solution.py:240
  12.9 1.0 %correlate.1 = bf16[2,2,128,128]{3,2,1,0:T(8,128)(2,1)} custom-call(bf16[16,2,16,128]{3,2,1,0:T(8,128)(2,1)S(1)} %channelize.1.recv), custom_call_target="tpu_custom_call" | custom-call | tf_op jit(solution)/shard_map/correlate/pallas_call | solution.py:265

commit v7 on v5

--- a/solution.py
+++ b/solution.py
@@ -99,10 +99,9 @@
     )
 
     def weigh(b):
-        values = table_v[b].astype(jnp.float32)
         for h in range(2):
             lanes = slice(h * 2 * COLS, (h + 1) * 2 * COLS)
-            weights[b, :, lanes] = (values * spread_taps[:, lanes]).astype(jnp.bfloat16)
+            weights[b, :, lanes] = table_v[b] * spread_taps[:, lanes].astype(jnp.bfloat16)
 
     for_each(blocks, weigh)
 
@@ -127,9 +126,14 @@
             load(h * HALF_FRAMES + first, count, sample_sem.at[h, index]).wait()
 
         def multiply(b):
-            rows = pl.ds(pl.multiple_of(h * HALF_ROWS, HALF_ROWS), HALF_ROWS)
-            values = x[pl.ds(h * HALF_FRAMES, HALF_FRAMES)].reshape(HALF_ROWS, NFFT)
-            prod[b, rows, :] = jnp.dot(values, weights[b], preferred_element_type=jnp.float32)
+            step = HALF_FRAMES // 2
+
+            @pl.loop(0, HALF_FRAMES // step)
+            def _(tile):
+                first = h * HALF_FRAMES + tile * step
+                values = x[pl.ds(first, step)].reshape(step * INP_DEV, NFFT)
+                rows = pl.ds(pl.multiple_of(first * INP_DEV, INP_DEV), step * INP_DEV)
+                prod[b, rows, :] = jnp.dot(values, weights[b], preferred_element_type=jnp.float32)
 
         for_each(blocks, multiply)
 
@@ -154,7 +158,8 @@
                     to = ((k % 4) * 4 + 2 * p + k // 4) * BLOCK
                     turned[to : to + BLOCK, :] = pair[k * BLOCK : (k + 1) * BLOCK, :]
             first = lax.broadcasted_iota(jnp.int32, (INP_DEV, 128), 1) < HALF
-            for g in range(BLOCK):
+            @pl.loop(0, BLOCK, unroll=4)
+            def _(g):
                 real = turned[pl.ds(g, 8, stride=BLOCK), :]
                 imag = turned[pl.ds(8 * BLOCK + g, 8, stride=BLOCK), :]
                 send[b * BLOCK + g, h] = jnp.concatenate(

time: 13.1 us -> 13.8 us (1.053)
  Pallas kernels: 13 us -> 13.7 us
    pallas_call x1, Pallas kernels: 12.1 us -> 12.7 us  [per_device(): pl.pallas_call(functools.partial(kernel, groups), out_shape=pltpu.VMEM((g...]
where the time goes in v7:
time: 13.8 us; the launch traced here: 13.7 us
  Pallas kernels  13.7 us (99%)
    pallas_call x1, Pallas kernels, per_device(): pl.pallas_call(functools.partial(kernel, groups), out_shape=pltpu.VMEM((g...  12.7 us
    pallas_call x1, Pallas kernels, per_device(): pl.pallas_call(correlate_kernel, out_shape=jax.ShapeDtypeStruct((CH_DEV,...  0.94 us

profile of v7, /device:TPU:0, one launch (start us, length us, event | category | flops | bytes accessed | tf_op | source)
XLA Modules:
  0.0 13.7 jit_solution(7515685865258763409)
XLA Ops:
  0.0 12.7 %channelize.1.recv = bf16[16,2,16,128]{3,2,1,0:T(8,128)(2,1)S(1)} custom-call(bf16[131,8,2048]{2,1,0:T(8,128)(2,1)} %bitcast.3, s32[4,2048]{1,0:T(4,128)} %taps.1, bf16[1,2048,128]{2,1,0:T(8,128)(2,1)} %constant.2.clone.table), custom_call_target="tpu_custom_call" | custom-call | tf_op jit(solution)/shard_map/channelize/pallas_call | solution.py:236
  12.8 0.9 %correlate.1 = bf16[2,2,128,128]{3,2,1,0:T(8,128)(2,1)} custom-call(bf16[16,2,16,128]{3,2,1,0:T(8,128)(2,1)S(1)} %channelize.1.recv), custom_call_target="tpu_custom_call" | custom-call | tf_op jit(solution)/shard_map/correlate/pallas_call | solution.py:261

commit v8 on v6

--- a/solution.py
+++ b/solution.py
@@ -22,7 +22,6 @@
 HALF_FRAMES = 68
 HALF_ROWS = HALF_FRAMES * INP_DEV
 LATE_FRAMES = FRAMES - HALF_FRAMES
-LOADS = ((0, 32), (32, LATE_FRAMES - 32))
 BLOCK_ROWS = CH_DEV * INP_DEV
 
 
@@ -65,16 +64,16 @@
     taps_copy.start()
     table_copy.start()
 
-    def load(first, count, sem):
-        part = pl.ds(first, count)
-        return pltpu.make_async_copy(samples.at[part], x.at[part], sem)
-
-    extra = load(LATE_FRAMES, HALF_FRAMES - LATE_FRAMES, load_sem.at[2])
+    def load(h, part):
+        frames = pl.ds(h * HALF_FRAMES, (HALF_FRAMES, LATE_FRAMES)[h])
+        span = pl.ds(part * (NFFT // 2), NFFT // 2)
+        return pltpu.make_async_copy(
+            samples.at[frames, :, span], x.at[frames, :, span], sample_sem.at[h, part]
+        )
+
     for h in range(2):
-        for index, (first, count) in enumerate(LOADS):
-            load(h * HALF_FRAMES + first, count, sample_sem.at[h, index]).start()
-        if h == 0:
-            extra.start()
+        for part in range(2):
+            load(h, part).start()
 
     barrier = pltpu.get_barrier_semaphore()
 
@@ -92,21 +91,23 @@
     taps_copy.wait()
     table_copy.wait()
 
-    tap_rows = taps_v[...].astype(jnp.float32)
-    tap_rows = jnp.concatenate([tap_rows, jnp.zeros_like(tap_rows)], axis=0).astype(jnp.bfloat16)
-    spread_taps = lax.dot_general(
-        tap_rows, spread, (((0,), (0,)), ((), ())), preferred_element_type=jnp.float32
-    )
-
-    def weigh(b):
-        values = table_v[b].astype(jnp.float32)
-        for h in range(2):
-            lanes = slice(h * 2 * COLS, (h + 1) * 2 * COLS)
-            weights[b, :, lanes] = (values * spread_taps[:, lanes]).astype(jnp.bfloat16)
-
-    for_each(blocks, weigh)
-
-    extra.wait()
+    depth = NFFT // 2
+
+    def weigh_part(part):
+        rows = slice(part * depth, (part + 1) * depth)
+        tap_rows = taps_v[:, rows].astype(jnp.float32)
+        tap_rows = jnp.concatenate([tap_rows, jnp.zeros_like(tap_rows)], axis=0)
+        spread_taps = lax.dot_general(
+            tap_rows.astype(jnp.bfloat16), spread, (((0,), (0,)), ((), ())),
+            preferred_element_type=jnp.float32,
+        ).astype(jnp.bfloat16)
+
+        def weigh(b):
+            for h in range(2):
+                lanes = slice(h * 2 * COLS, (h + 1) * 2 * COLS)
+                weights[b, rows, lanes] = table_v[b, rows, :] * spread_taps[:, lanes]
+
+        for_each(blocks, weigh)
 
     def transfer(peer, source, target):
         return pltpu.make_async_remote_copy(
@@ -121,14 +122,16 @@
     def own(h):
         return pltpu.make_async_copy(send.at[me, h], recv.at[me, h], own_sem.at[h])
 
-    def multiply_half(h):
-        for index, (first, count) in enumerate(LOADS):
-            load(h * HALF_FRAMES + first, count, sample_sem.at[h, index]).wait()
-
+    def multiply_part(h, part):
         def multiply(b):
             rows = pl.ds(h * HALF_ROWS, HALF_ROWS)
-            values = x[pl.ds(h * HALF_FRAMES, HALF_FRAMES)].reshape(HALF_ROWS, NFFT)
-            prod[b, rows, :] = jnp.dot(values, weights[b], preferred_element_type=jnp.float32)
+            span = slice(part * depth, (part + 1) * depth)
+            values = x[pl.ds(h * HALF_FRAMES, HALF_FRAMES), :, span].reshape(HALF_ROWS, depth)
+            product = jnp.dot(values, weights[b, span, :], preferred_element_type=jnp.float32)
+            if part == 0:
+                prod[b, rows, :] = product
+            else:
+                prod[b, rows, :] += product
 
         for_each(blocks, multiply)
 
@@ -175,11 +178,19 @@
         for_each_peer(groups, start)
         own(h).start()
 
-    multiply_half(0)
-    multiply_half(1)
+    weigh_part(0)
+    load(0, 0).wait()
+    multiply_part(0, 0)
+    weigh_part(1)
+    load(0, 1).wait()
+    multiply_part(0, 1)
+    load(1, 0).wait()
+    multiply_part(1, 0)
     turn_half(0)
     pl.semaphore_wait(barrier, groups - 1)
     send_half(0)
+    load(1, 1).wait()
+    multiply_part(1, 1)
     turn_half(1)
     send_half(1)
 
@@ -251,8 +262,8 @@
             pltpu.VMEM((HALF * INP_DEV, 128), f32),
             pltpu.VMEM((BLOCK_ROWS * BLOCK, 128), f32),
             pltpu.VMEM((groups, 2, BLOCK_ROWS, 128), bf16),
-            pltpu.SemaphoreType.DMA((3,)),
-            pltpu.SemaphoreType.DMA((2, len(LOADS))),
+            pltpu.SemaphoreType.DMA((2,)),
+            pltpu.SemaphoreType.DMA((2, 2)),
             pltpu.SemaphoreType.DMA((2,)),
             pltpu.SemaphoreType.DMA,
             pltpu.SemaphoreType.DMA,

time: 14 us -> 14.5 us (1.036)
  Pallas kernels: 13.8 us -> 14.3 us
    pallas_call x1, Pallas kernels: 12.9 us -> 13.4 us  [per_device(): pl.pallas_call(functools.partial(kernel, groups), out_shape=pltpu.VMEM((g...]
where the time goes in v8:
time: 14.5 us; the launch traced here: 14.4 us
  Pallas kernels  14.3 us (99%)
    pallas_call x1, Pallas kernels, per_device(): pl.pallas_call(functools.partial(kernel, groups), out_shape=pltpu.VMEM((g...  13.4 us
    pallas_call x1, Pallas kernels, per_device(): pl.pallas_call(correlate_kernel, out_shape=jax.ShapeDtypeStruct((CH_DEV,...  0.95 us

profile of v8, /device:TPU:0, one launch (start us, length us, event | category | flops | bytes accessed | tf_op | source)
XLA Modules:
  0.0 14.4 jit_solution(15245933975495164974)
XLA Ops:
  0.0 13.4 %channelize.1.recv = bf16[16,2,16,128]{3,2,1,0:T(8,128)(2,1)S(1)} custom-call(bf16[131,8,2048]{2,1,0:T(8,128)(2,1)} %bitcast.3, s32[4,2048]{1,0:T(4,128)} %taps.1, bf16[1,2048,128]{2,1,0:T(8,128)(2,1)} %constant.2.clone.table), custom_call_target="tpu_custom_call" | custom-call | tf_op jit(solution)/shard_map/channelize/pallas_call | solution.py:251
  13.4 0.9 %correlate.1 = bf16[2,2,128,128]{3,2,1,0:T(8,128)(2,1)} custom-call(bf16[16,2,16,128]{3,2,1,0:T(8,128)(2,1)S(1)} %channelize.1.recv), custom_call_target="tpu_custom_call" | custom-call | tf_op jit(solution)/shard_map/correlate/pallas_call | solution.py:276

commit v9 on v5

--- a/solution.py
+++ b/solution.py
@@ -46,11 +46,7 @@
 
 
 def for_each_peer(groups, body):
-    if groups <= BLOCK:
-        for step in range(1, groups):
-            body(step)
-    else:
-        pl.loop(1, groups)(body)
+    pl.loop(1, groups, unroll=3 if groups <= BLOCK else 1)(body)
 
 
 def kernel(
@@ -92,19 +88,24 @@
     taps_copy.wait()
     table_copy.wait()
 
-    tap_rows = taps_v[...].astype(jnp.float32)
-    tap_rows = jnp.concatenate([tap_rows, jnp.zeros_like(tap_rows)], axis=0).astype(jnp.bfloat16)
-    spread_taps = lax.dot_general(
-        tap_rows, spread, (((0,), (0,)), ((), ())), preferred_element_type=jnp.float32
-    )
-
-    def weigh(b):
-        values = table_v[b].astype(jnp.float32)
-        for h in range(2):
-            lanes = slice(h * 2 * COLS, (h + 1) * 2 * COLS)
-            weights[b, :, lanes] = (values * spread_taps[:, lanes]).astype(jnp.bfloat16)
-
-    for_each(blocks, weigh)
+    depth = NFFT // 4
+
+    @pl.loop(0, NFFT // depth)
+    def _(tile):
+        rows = pl.ds(pl.multiple_of(tile * depth, depth), depth)
+        tap_rows = taps_v[:, rows].astype(jnp.float32)
+        tap_rows = jnp.concatenate([tap_rows, jnp.zeros_like(tap_rows)], axis=0)
+        spread_taps = lax.dot_general(
+            tap_rows.astype(jnp.bfloat16), spread, (((0,), (0,)), ((), ())),
+            preferred_element_type=jnp.float32,
+        ).astype(jnp.bfloat16)
+
+        def weigh(b):
+            for h in range(2):
+                lanes = slice(h * 2 * COLS, (h + 1) * 2 * COLS)
+                weights[b, rows, lanes] = table_v[b, rows, :] * spread_taps[:, lanes]
+
+        for_each(blocks, weigh)
 
     extra.wait()
 
@@ -154,7 +155,8 @@
                     to = ((k % 4) * 4 + 2 * p + k // 4) * BLOCK
                     turned[to : to + BLOCK, :] = pair[k * BLOCK : (k + 1) * BLOCK, :]
             first = lax.broadcasted_iota(jnp.int32, (INP_DEV, 128), 1) < HALF
-            for g in range(BLOCK):
+            @pl.loop(0, BLOCK, unroll=4)
+            def _(g):
                 real = turned[pl.ds(g, 8, stride=BLOCK), :]
                 imag = turned[pl.ds(8 * BLOCK + g, 8, stride=BLOCK), :]
                 send[b * BLOCK + g, h] = jnp.concatenate(
@@ -193,8 +195,9 @@
     shape = (recv.shape[0], INP_DEV, 128)
     upper = lax.broadcasted_iota(jnp.int32, shape, 1) < 4
     first = lax.broadcasted_iota(jnp.int32, (inputs, 128), 1) < HALF
-    for h in range(2):
-        lanes = slice(h * 128, (h + 1) * 128)
+    @pl.loop(0, 2)
+    def _(h):
+        lanes = pl.ds(pl.multiple_of(h * 128, 128), 128)
         early = recv[:, h, 0:INP_DEV, :].astype(jnp.float32)
         late = recv[:, h, INP_DEV:, :].astype(jnp.float32)
         by_channel = (
@@ -209,13 +212,16 @@
 
     def correlate(tile):
         rows = pl.ds(tile * 128, 128)
-        for q in range(CH_DEV):
-            for r in range(2):
-                product = lax.dot_general(
-                    stack[q, r, rows, :], stack[q, 0], (((1,), (1,)), ((), ())),
-                    preferred_element_type=jnp.float32,
-                )
-                out[q, r, rows, :] = (product * norm).astype(jnp.bfloat16)
+
+        @pl.loop(0, CH_DEV)
+        def _(q):
+            left = jnp.concatenate([stack[q, 0, rows, :], stack[q, 1, rows, :]], axis=0)
+            product = lax.dot_general(
+                left, stack[q, 0], (((1,), (1,)), ((), ())), preferred_element_type=jnp.float32
+            )
+            product = (product * norm).astype(jnp.bfloat16)
+            out[q, 0, rows, :] = product[:128]
+            out[q, 1, rows, :] = product[128:]
 
     for_each(inputs // 128, correlate)
 

time: 13.1 us -> 14.4 us (1.099)
  Pallas kernels: 13 us -> 14.2 us
    pallas_call x1, Pallas kernels: 12.1 us -> 13 us  [per_device(): pl.pallas_call(functools.partial(kernel, groups), out_shape=pltpu.VMEM((g...]
    pallas_call x1, Pallas kernels: 0.94 us -> 1.23 us  [per_device(): pl.pallas_call(correlate_kernel, out_shape=jax.ShapeDtypeStruct((CH_DEV,...]
where the time goes in v9:
time: 14.4 us; the launch traced here: 14.2 us
  Pallas kernels  14.2 us (99%)
    pallas_call x1, Pallas kernels, per_device(): pl.pallas_call(functools.partial(kernel, groups), out_shape=pltpu.VMEM((g...  13 us
    pallas_call x1, Pallas kernels, per_device(): pl.pallas_call(correlate_kernel, out_shape=jax.ShapeDtypeStruct((CH_DEV,...  1.23 us

profile of v9, /device:TPU:0, one launch (start us, length us, event | category | flops | bytes accessed | tf_op | source)
XLA Modules:
  0.0 14.2 jit_solution(12274393572765627297)
XLA Ops:
  0.0 13.0 %channelize.1.recv = bf16[16,2,16,128]{3,2,1,0:T(8,128)(2,1)S(1)} custom-call(bf16[131,8,2048]{2,1,0:T(8,128)(2,1)} %bitcast.3, s32[4,2048]{1,0:T(4,128)} %taps.1, bf16[1,2048,128]{2,1,0:T(8,128)(2,1)} %constant.2.clone.table), custom_call_target="tpu_custom_call" | custom-call | tf_op jit(solution)/shard_map/channelize/pallas_call | solution.py:237
  13.0 1.2 %correlate.1 = bf16[2,2,128,128]{3,2,1,0:T(8,128)(2,1)} custom-call(bf16[16,2,16,128]{3,2,1,0:T(8,128)(2,1)S(1)} %channelize.1.recv), custom_call_target="tpu_custom_call" | custom-call | tf_op jit(solution)/shard_map/correlate/pallas_call | solution.py:262

commit v10 on v5

--- a/solution.py
+++ b/solution.py
@@ -117,9 +117,6 @@
             device_id={"inp": peer},
             device_id_type=pl.DeviceIdType.MESH,
         )
-
-    def own(h):
-        return pltpu.make_async_copy(send.at[me, h], recv.at[me, h], own_sem.at[h])
 
     @pl.loop(0, 2)
     def _(h):
@@ -167,20 +164,16 @@
 
         for_each(blocks, turn)
 
-        @pl.when(h == 0)
-        def _():
-            pl.semaphore_wait(barrier, groups - 1)
-
-        def start(step):
-            peer = lax.rem(me + step, groups)
-            transfer(peer, send.at[peer, h], recv.at[me, h]).start()
-
-        for_each_peer(groups, start)
-
-        own(h).start()
-
-    for h in range(2):
-        own(h).wait()
+    pl.semaphore_wait(barrier, groups - 1)
+
+    def start(step):
+        peer = lax.rem(me + step, groups)
+        transfer(peer, send.at[peer], recv.at[me]).start()
+
+    for_each_peer(groups, start)
+    own = pltpu.make_async_copy(send.at[me], recv.at[me], own_sem)
+    own.start()
+    own.wait()
     others = pl.ds(0, groups - 1)
     everything = transfer(lax.rem(me + 1, groups), send.at[others], recv.at[others])
     everything.wait_recv()
@@ -244,7 +237,7 @@
             pltpu.VMEM((groups, 2, BLOCK_ROWS, 128), bf16),
             pltpu.SemaphoreType.DMA((3,)),
             pltpu.SemaphoreType.DMA((2, len(LOADS))),
-            pltpu.SemaphoreType.DMA((2,)),
+            pltpu.SemaphoreType.DMA,
             pltpu.SemaphoreType.DMA,
             pltpu.SemaphoreType.DMA,
         ],

time: 13.1 us -> 13.1 us (level)
  no operation moved by 1% of the time
where the time goes in v10:
time: 13.1 us; the launch traced here: 13 us
  Pallas kernels  13 us (99%)
    pallas_call x1, Pallas kernels, per_device(): pl.pallas_call(functools.partial(kernel, groups), out_shape=pltpu.VMEM((g...  12 us
    pallas_call x1, Pallas kernels, per_device(): pl.pallas_call(correlate_kernel, out_shape=jax.ShapeDtypeStruct((CH_DEV,...  0.94 us

profile of v10, /device:TPU:0, one launch (start us, length us, event | category | flops | bytes accessed | tf_op | source)
XLA Modules:
  0.0 13.0 jit_solution(11807584284152841317)
XLA Ops:
  0.0 12.0 %channelize.1.recv = bf16[16,2,16,128]{3,2,1,0:T(8,128)(2,1)S(1)} custom-call(bf16[131,8,2048]{2,1,0:T(8,128)(2,1)} %bitcast.3, s32[4,2048]{1,0:T(4,128)} %taps.1, bf16[1,2048,128]{2,1,0:T(8,128)(2,1)} %constant.2.clone.table), custom_call_target="tpu_custom_call" | custom-call | tf_op jit(solution)/shard_map/channelize/pallas_call | solution.py:224
  12.0 0.9 %correlate.1 = bf16[2,2,128,128]{3,2,1,0:T(8,128)(2,1)} custom-call(bf16[16,2,16,128]{3,2,1,0:T(8,128)(2,1)S(1)} %channelize.1.recv), custom_call_target="tpu_custom_call" | custom-call | tf_op jit(solution)/shard_map/correlate/pallas_call | solution.py:249

commit v11 on v10

--- a/solution.py
+++ b/solution.py
@@ -18,12 +18,11 @@
 FRAMES = SPEC + TAPS - 1
 BLOCK = 16
 COLS = BLOCK * CH_DEV * 2
-HALF = SPEC // 2
 HALF_FRAMES = 68
 HALF_ROWS = HALF_FRAMES * INP_DEV
 LATE_FRAMES = FRAMES - HALF_FRAMES
 LOADS = ((0, 32), (32, LATE_FRAMES - 32))
-BLOCK_ROWS = CH_DEV * INP_DEV
+BLOCK_ROWS = CH_DEV * 2 * INP_DEV
 
 
 def dft_table(groups):
@@ -31,10 +30,10 @@
     block = np.arange(groups // BLOCK)[:, None, None]
     column = np.arange(2 * COLS)[None, None, :] % COLS
     part = column // BLOCK
-    channel = FIRST_CH + (block * BLOCK + column % BLOCK) * CH_DEV + part % CH_DEV
+    channel = FIRST_CH + (block * BLOCK + column % BLOCK) * CH_DEV + part // 2
     phase = (n * channel % NFFT).astype(np.float32) * np.float32(2.0 * math.pi / NFFT)
     phase = phase.astype(np.float64)
-    table = np.where(part < CH_DEV, np.cos(phase), -np.sin(phase)).astype(np.float32)
+    table = np.where(part % 2 == 0, np.cos(phase), -np.sin(phase)).astype(np.float32)
     return (table * np.float32(2.0**-19)).astype(jnp.bfloat16)
 
 
@@ -130,39 +129,22 @@
 
         for_each(blocks, multiply)
 
-        def turn(b):
-            count = HALF * INP_DEV
-            start = pl.multiple_of(h * count, count)
-            half = (
-                prod[b, pl.ds(start, count + INP_DEV), 0:128]
-                + prod[b, pl.ds(start + 2 * INP_DEV, count + INP_DEV), 128:256]
-            )
-            volts[...] = half[:count] + pltpu.roll(half[INP_DEV:], COLS, 1)
-            low_lanes = lax.broadcasted_iota(jnp.int32, (HALF, 128), 1) < COLS
-            for p in range(2):
-                rows = []
-                for ia in range(2):
-                    i = 4 * ia + 2 * p
-                    low = volts[pl.ds(i, HALF, stride=INP_DEV), :]
-                    high = volts[pl.ds(i + 1, HALF, stride=INP_DEV), :]
-                    rows.append(jnp.where(low_lanes, low, pltpu.roll(high, COLS, 1)))
-                pair = jnp.concatenate(rows, axis=0).T
-                for k in range(8):
-                    to = ((k % 4) * 4 + 2 * p + k // 4) * BLOCK
-                    turned[to : to + BLOCK, :] = pair[k * BLOCK : (k + 1) * BLOCK, :]
-            first = lax.broadcasted_iota(jnp.int32, (INP_DEV, 128), 1) < HALF
-            for g in range(BLOCK):
-                real = turned[pl.ds(g, 8, stride=BLOCK), :]
-                imag = turned[pl.ds(8 * BLOCK + g, 8, stride=BLOCK), :]
-                send[b * BLOCK + g, h] = jnp.concatenate(
-                    [
-                        jnp.where(first, real, pltpu.roll(imag, HALF, 1)),
-                        jnp.where(first, pltpu.roll(real, HALF, 1), imag),
-                    ],
-                    axis=0,
-                ).astype(jnp.bfloat16)
-
-        for_each(blocks, turn)
+    def turn(b):
+        count = SPEC * INP_DEV
+        half = prod[b, 0 : count + INP_DEV, 0:128] + prod[b, 16 : count + 24, 128:256]
+        volts[...] = half[:count] + pltpu.roll(half[INP_DEV:], COLS, 1)
+        lane = lax.broadcasted_iota(jnp.int32, (SPEC, 128), 1)
+        for i in range(INP_DEV // 2):
+            low = volts[pl.ds(i, SPEC, stride=INP_DEV), :]
+            high = volts[pl.ds(i + 4, SPEC, stride=INP_DEV), :]
+            pair = jnp.where(lane < COLS, low, pltpu.roll(high, COLS, 1)).T
+            for k in range(8):
+                to = (k % 4) * INP_DEV * BLOCK + (i + 4 * (k // 4)) * BLOCK
+                turned[to : to + BLOCK, :] = pair[k * BLOCK : (k + 1) * BLOCK, :]
+        for g in range(BLOCK):
+            send[b * BLOCK + g] = turned[pl.ds(g, BLOCK_ROWS, stride=BLOCK), :].astype(jnp.bfloat16)
+
+    for_each(blocks, turn)
 
     pl.semaphore_wait(barrier, groups - 1)
 
@@ -183,25 +165,16 @@
 def correlate_kernel(recv, out, stack):
     inputs = recv.shape[0] * INP_DEV
     norm = 1.0 / math.sqrt(SPEC)
-    shape = (recv.shape[0], INP_DEV, 128)
-    upper = lax.broadcasted_iota(jnp.int32, shape, 1) < 4
-    first = lax.broadcasted_iota(jnp.int32, (inputs, 128), 1) < HALF
-    for h in range(2):
-        lanes = slice(h * 128, (h + 1) * 128)
-        early = recv[:, h, 0:INP_DEV, :].astype(jnp.float32)
-        late = recv[:, h, INP_DEV:, :].astype(jnp.float32)
-        by_channel = (
-            jnp.where(upper, early, pltpu.roll(late, 4, 1)),
-            jnp.where(upper, pltpu.roll(early, 4, 1), late),
-        )
-        for q in range(CH_DEV):
-            values = by_channel[q].reshape(inputs, 128)
-            rolled = pltpu.roll(values, HALF, 1)
-            stack[q, 0, :, lanes] = values.astype(jnp.bfloat16)
-            stack[q, 1, :, lanes] = jnp.where(first, rolled, -rolled).astype(jnp.bfloat16)
+    for q in range(CH_DEV):
+        for r in range(2):
+            at = (2 * q + r) * INP_DEV
+            values = recv[:, at : at + INP_DEV, :].astype(jnp.float32).reshape(inputs, SPEC)
+            stack[q, 0, :, r * SPEC : (r + 1) * SPEC] = values.astype(jnp.bfloat16)
+            turned_part = values if r == 1 else -values
+            stack[q, 1, :, (1 - r) * SPEC : (2 - r) * SPEC] = turned_part.astype(jnp.bfloat16)
 
     def correlate(tile):
-        rows = pl.ds(tile * 128, 128)
+        rows = pl.ds(tile * SPEC, SPEC)
         for q in range(CH_DEV):
             for r in range(2):
                 product = lax.dot_general(
@@ -210,7 +183,7 @@
                 )
                 out[q, r, rows, :] = (product * norm).astype(jnp.bfloat16)
 
-    for_each(inputs // 128, correlate)
+    for_each(inputs // SPEC, correlate)
 
 
 def per_device(samples, taps):
@@ -223,7 +196,7 @@
     bf16, f32 = jnp.bfloat16, jnp.float32
     gathered = pl.pallas_call(
         functools.partial(kernel, groups),
-        out_shape=pltpu.VMEM((groups, 2, BLOCK_ROWS, 128), bf16),
+        out_shape=pltpu.VMEM((groups, BLOCK_ROWS, SPEC), bf16),
         in_specs=[pl.BlockSpec(memory_space=pltpu.HBM)] * 3,
         out_specs=pl.BlockSpec(memory_space=pltpu.VMEM),
         scratch_shapes=[
@@ -232,9 +205,9 @@
             pltpu.VMEM((blocks, NFFT, 2 * COLS), bf16),
             pltpu.VMEM((blocks, NFFT, TAPS * COLS), bf16),
             pltpu.VMEM((blocks, 2 * HALF_ROWS, TAPS * COLS), f32),
-            pltpu.VMEM((HALF * INP_DEV, 128), f32),
-            pltpu.VMEM((BLOCK_ROWS * BLOCK, 128), f32),
-            pltpu.VMEM((groups, 2, BLOCK_ROWS, 128), bf16),
+            pltpu.VMEM((SPEC * INP_DEV, 128), f32),
+            pltpu.VMEM((BLOCK_ROWS * BLOCK, SPEC), f32),
+            pltpu.VMEM((groups, BLOCK_ROWS, SPEC), bf16),
             pltpu.SemaphoreType.DMA((3,)),
             pltpu.SemaphoreType.DMA((2, len(LOADS))),
             pltpu.SemaphoreType.DMA,

time: 13.1 us -> 12.7 us (0.969)
  Pallas kernels: 13 us -> 12.5 us
    pallas_call x1, Pallas kernels: 12 us -> 11.6 us  [per_device(): pl.pallas_call(functools.partial(kernel, groups), out_shape=pltpu.VMEM((g...]
where the time goes in v11:
time: 12.7 us; the launch traced here: 12.6 us
  Pallas kernels  12.5 us (98%)
    pallas_call x1, Pallas kernels, per_device(): pl.pallas_call(functools.partial(kernel, groups), out_shape=pltpu.VMEM((g...  11.6 us
    pallas_call x1, Pallas kernels, per_device(): pl.pallas_call(correlate_kernel, out_shape=jax.ShapeDtypeStruct((CH_DEV,...  0.9 us

profile of v11, /device:TPU:0, one launch (start us, length us, event | category | flops | bytes accessed | tf_op | source)
XLA Modules:
  0.0 12.6 jit_solution(17111673292699560427)
XLA Ops:
  0.0 11.6 %channelize.1.recv = bf16[16,32,128]{2,1,0:T(8,128)(2,1)S(1)} custom-call(bf16[131,8,2048]{2,1,0:T(8,128)(2,1)} %bitcast.3, s32[4,2048]{1,0:T(4,128)} %taps.1, bf16[1,2048,128]{2,1,0:T(8,128)(2,1)} %constant.2.clone.table), custom_call_target="tpu_custom_call" | custom-call | tf_op jit(solution)/shard_map/channelize/pallas_call | solution.py:197
  11.7 0.9 %correlate.1 = bf16[2,2,128,128]{3,2,1,0:T(8,128)(2,1)} custom-call(bf16[16,32,128]{2,1,0:T(8,128)(2,1)S(1)} %channelize.1.recv), custom_call_target="tpu_custom_call" | custom-call | tf_op jit(solution)/shard_map/correlate/pallas_call | solution.py:222

commit v12 on v11

--- a/solution.py
+++ b/solution.py
@@ -21,7 +21,7 @@
 HALF_FRAMES = 68
 HALF_ROWS = HALF_FRAMES * INP_DEV
 LATE_FRAMES = FRAMES - HALF_FRAMES
-LOADS = ((0, 32), (32, LATE_FRAMES - 32))
+LOADS = tuple((first, min(8, LATE_FRAMES - first)) for first in range(0, LATE_FRAMES, 8))
 BLOCK_ROWS = CH_DEV * 2 * INP_DEV
 
 
@@ -141,8 +141,13 @@
             for k in range(8):
                 to = (k % 4) * INP_DEV * BLOCK + (i + 4 * (k // 4)) * BLOCK
                 turned[to : to + BLOCK, :] = pair[k * BLOCK : (k + 1) * BLOCK, :]
-        for g in range(BLOCK):
-            send[b * BLOCK + g] = turned[pl.ds(g, BLOCK_ROWS, stride=BLOCK), :].astype(jnp.bfloat16)
+        if blocks > 1:
+            for g in range(BLOCK):
+                fill(b * BLOCK + g, g)
+
+    def fill(group, g):
+        rows = turned[pl.ds(g, BLOCK_ROWS, stride=BLOCK), :]
+        send[group] = rows.astype(jnp.bfloat16)
 
     for_each(blocks, turn)
 
@@ -150,9 +155,13 @@
 
     def start(step):
         peer = lax.rem(me + step, groups)
+        if blocks == 1:
+            fill(peer, peer)
         transfer(peer, send.at[peer], recv.at[me]).start()
 
     for_each_peer(groups, start)
+    if blocks == 1:
+        fill(me, me)
     own = pltpu.make_async_copy(send.at[me], recv.at[me], own_sem)
     own.start()
     own.wait()

time: 12.7 us -> 13 us (1.024)
  Pallas kernels: 12.5 us -> 12.9 us
    pallas_call x1, Pallas kernels: 11.6 us -> 12 us  [per_device(): pl.pallas_call(functools.partial(kernel, groups), out_shape=pltpu.VMEM((g...]
where the time goes in v12:
time: 13 us; the launch traced here: 12.9 us
  Pallas kernels  12.9 us (99%)
    pallas_call x1, Pallas kernels, per_device(): pl.pallas_call(functools.partial(kernel, groups), out_shape=pltpu.VMEM((g...  12 us
    pallas_call x1, Pallas kernels, per_device(): pl.pallas_call(correlate_kernel, out_shape=jax.ShapeDtypeStruct((CH_DEV,...  0.9 us

profile of v12, /device:TPU:0, one launch (start us, length us, event | category | flops | bytes accessed | tf_op | source)
XLA Modules:
  0.0 12.9 jit_solution(3633878966923637316)
XLA Ops:
  0.0 12.0 %channelize.1.recv = bf16[16,32,128]{2,1,0:T(8,128)(2,1)S(1)} custom-call(bf16[131,8,2048]{2,1,0:T(8,128)(2,1)} %bitcast.3, s32[4,2048]{1,0:T(4,128)} %taps.1, bf16[1,2048,128]{2,1,0:T(8,128)(2,1)} %constant.2.clone.table), custom_call_target="tpu_custom_call" | custom-call | tf_op jit(solution)/shard_map/channelize/pallas_call | solution.py:206
  12.0 0.9 %correlate.1 = bf16[2,2,128,128]{3,2,1,0:T(8,128)(2,1)} custom-call(bf16[16,32,128]{2,1,0:T(8,128)(2,1)S(1)} %channelize.1.recv), custom_call_target="tpu_custom_call" | custom-call | tf_op jit(solution)/shard_map/correlate/pallas_call | solution.py:231

commit v13 on v11

--- a/solution.py
+++ b/solution.py
@@ -95,13 +95,12 @@
     tap_rows = jnp.concatenate([tap_rows, jnp.zeros_like(tap_rows)], axis=0).astype(jnp.bfloat16)
     spread_taps = lax.dot_general(
         tap_rows, spread, (((0,), (0,)), ((), ())), preferred_element_type=jnp.float32
-    )
+    ).astype(jnp.bfloat16)
 
     def weigh(b):
-        values = table_v[b].astype(jnp.float32)
         for h in range(2):
             lanes = slice(h * 2 * COLS, (h + 1) * 2 * COLS)
-            weights[b, :, lanes] = (values * spread_taps[:, lanes]).astype(jnp.bfloat16)
+            weights[b, :, lanes] = table_v[b] * spread_taps[:, lanes]
 
     for_each(blocks, weigh)
 

time: 12.7 us -> 12.7 us (level)
  no operation moved by 1% of the time
where the time goes in v13:
time: 12.7 us; the launch traced here: 12.6 us
  Pallas kernels  12.5 us (98%)
    pallas_call x1, Pallas kernels, per_device(): pl.pallas_call(functools.partial(kernel, groups), out_shape=pltpu.VMEM((g...  11.6 us
    pallas_call x1, Pallas kernels, per_device(): pl.pallas_call(correlate_kernel, out_shape=jax.ShapeDtypeStruct((CH_DEV,...  0.9 us

profile of v13, /device:TPU:0, one launch (start us, length us, event | category | flops | bytes accessed | tf_op | source)
XLA Modules:
  0.0 12.6 jit_solution(6789222035305027860)
XLA Ops:
  0.0 11.6 %channelize.1.recv = bf16[16,32,128]{2,1,0:T(8,128)(2,1)S(1)} custom-call(bf16[131,8,2048]{2,1,0:T(8,128)(2,1)} %bitcast.3, s32[4,2048]{1,0:T(4,128)} %taps.1, bf16[1,2048,128]{2,1,0:T(8,128)(2,1)} %constant.2.clone.table), custom_call_target="tpu_custom_call" | custom-call | tf_op jit(solution)/shard_map/channelize/pallas_call | solution.py:196
  11.7 0.9 %correlate.1 = bf16[2,2,128,128]{3,2,1,0:T(8,128)(2,1)} custom-call(bf16[16,32,128]{2,1,0:T(8,128)(2,1)S(1)} %channelize.1.recv), custom_call_target="tpu_custom_call" | custom-call | tf_op jit(solution)/shard_map/correlate/pallas_call | solution.py:221
